TPU v7x, 32 devices: a whole 2x2x4 slice. The times are simulated.
32 devices in a mesh: dp: 16 (over z, y, core), ctx: 2 (over x).
Axes of the slice: x: 2, y: 2, z: 4, core: 2. Of those that a mesh axis runs over, the one named last changes fastest.
Arguments:
- events: bfloat16 [8192, 512], P(('dp', 'ctx')), may hold values from -6 to 6
- out_grad: bfloat16 [8192, 512], P(('dp', 'ctx')), may hold values from -6 to 6
- proj_weight: bfloat16 [512, 2048], replicated, may hold values from -0.25 to 0.25
- out_weight: bfloat16 [512, 512], replicated, may hold values from -0.25 to 0.25
- lengths: int32 [16, 4], P('dp'), may hold values from 1 to 256, 512 in all within a row
- tile_mask: int32 [64, 4], P('dp'), may hold values 0 or 1
- quotient_shard: int32 [8192], P(('dp', 'ctx')), may hold values from 0 to 31, as said below
- quotient_row: int32 [8192], P(('dp', 'ctx')), may hold values from 0 to 65535
- remainder_shard: int32 [8192], P(('dp', 'ctx')), may hold values from 0 to 31, as said below
- remainder_row: int32 [8192], P(('dp', 'ctx')), may hold values from 0 to 65535
Outputs:
- quotient_grads: float32 [12288, 512], P(('dp', 'ctx'))
- remainder_grads: float32 [12288, 512], P(('dp', 'ctx'))
- proj_weight_grad: float32 [512, 2048], replicated
- out_weight_grad: float32 [512, 512], replicated
Inputs may be any that keep to these rules, and one draw needn't show every extreme that they name: `quotient_shard`: in every device's 256 rows no shard is named more than 12 times, and some shard exactly 12 times. `remainder_shard`: in every device's 256 rows no shard is named more than 12 times, and some shard exactly 12 times.
All inputs are finite; a program needn't handle non-finite values. No bound on the sum of `tile_mask` on one device may be relied on, other than what follows from the above.
Results may differ from a plain program's by a relative error of at most 0.0068.
Values may be sent and summed in bfloat16 or wider, within the bound.
A program may use at most 128 MiB of HBM per device.

v0:
```python
import math

import jax
import jax.numpy as jnp
from jax import lax
from jax.sharding import PartitionSpec as P

HEADS = 8
TILE = 128


EPSILON = 1e-05


def passed_along(shard, axis, by):
    count = lax.axis_size(axis)
    pairs = [(i, i + by) for i in range(count) if 0 <= i + by < count]
    return lax.ppermute(shard, axis, pairs)


def from_behind(shard, axis, by):
    count = lax.axis_size(axis)
    return lax.ppermute(shard, axis, [(i, (i + by) % count) for i in range(count)])


def silu_grad(value, sigma):
    return sigma * (1.0 + value * (1.0 - sigma))


def visible_weight(history, tile_table, row_start, row_count, col_start, col_count, longest):
    row_pos = row_start + jnp.arange(row_count, dtype=jnp.int32)
    col_pos = col_start + jnp.arange(col_count, dtype=jnp.int32)
    doc_ends = jnp.cumsum(history)
    row_doc = jnp.sum((row_pos[:, None] >= doc_ends[None, :]).astype(jnp.int32), axis=1)
    col_doc = jnp.sum((col_pos[:, None] >= doc_ends[None, :]).astype(jnp.int32), axis=1)
    tile_ids = jnp.arange(tile_table.shape[0], dtype=jnp.int32)
    row_tiles = (row_pos[:, None] // TILE == tile_ids[None, :]).astype(jnp.float32)
    col_tiles = (col_pos[:, None] // TILE == tile_ids[None, :]).astype(jnp.float32)
    tile_rows = jnp.dot(row_tiles, tile_table.astype(jnp.float32), precision=lax.Precision.HIGHEST)
    tile_full = jnp.dot(tile_rows, col_tiles.T, precision=lax.Precision.HIGHEST)
    visible = (
        (row_doc[:, None] == col_doc[None, :])
        & (col_pos[None, :] <= row_pos[:, None])
        & (tile_full > 0.5)
    )
    return visible.astype(jnp.float32) / longest


def guarded(weight, compute, empty_result):
    return lax.cond(jnp.any(weight > 0.0), compute, lambda: empty_result)


def forward_block(query_heads, key_rows, value_rows, weight, score_scale):
    col_count = key_rows.shape[0]
    key_heads = key_rows.reshape(col_count, HEADS, -1)
    value_heads = value_rows.reshape(col_count, HEADS, -1)
    scores = (
        jnp.einsum("ihd,jhd->hij", query_heads, key_heads, preferred_element_type=jnp.float32)
        * score_scale
    )
    attention = (scores * jax.nn.sigmoid(scores) * weight[None]).astype(jnp.bfloat16)
    mixed_rows = jnp.einsum(
        "hij,jhd->ihd", attention, value_heads, preferred_element_type=jnp.float32
    )
    return mixed_rows.reshape(query_heads.shape[0], -1)


def backward_block(query_heads, grad_heads, key_rows, value_rows, weight, score_scale):
    col_count = key_rows.shape[0]
    row_count = query_heads.shape[0]
    key_heads = key_rows.reshape(col_count, HEADS, -1)
    value_heads = value_rows.reshape(col_count, HEADS, -1)
    scores = (
        jnp.einsum("ihd,jhd->hij", query_heads, key_heads, preferred_element_type=jnp.float32)
        * score_scale
    )
    sigmoid_scores = jax.nn.sigmoid(scores)
    attention = (scores * sigmoid_scores * weight[None]).astype(jnp.bfloat16)
    grad_attention = jnp.einsum(
        "ihd,jhd->hij", grad_heads, value_heads, preferred_element_type=jnp.float32
    )
    grad_scores = (grad_attention * weight[None] * silu_grad(scores, sigmoid_scores)).astype(
        jnp.bfloat16
    )
    grad_values = jnp.einsum(
        "hij,ihd->jhd", attention, grad_heads, preferred_element_type=jnp.float32
    ).reshape(col_count, -1)
    grad_query = (
        jnp.einsum(
            "hij,jhd->ihd", grad_scores, key_heads, preferred_element_type=jnp.float32
        ).reshape(row_count, -1)
        * score_scale
    )
    grad_keys = (
        jnp.einsum(
            "hij,ihd->jhd", grad_scores, query_heads, preferred_element_type=jnp.float32
        ).reshape(col_count, -1)
        * score_scale
    )
    return (grad_query, grad_keys, grad_values)


def pack_rows(grad_events, shards, table_rows, data_size, loop_size, capacity):
    row_count, model_width = grad_events.shape
    slot_count = data_size * loop_size * capacity
    earlier = jnp.arange(row_count)[None, :] < jnp.arange(row_count)[:, None]
    matches = (shards[:, None] == shards[None, :]) & earlier
    slot_rank = jnp.sum(matches.astype(jnp.int32), axis=1)
    target = shards * capacity + slot_rank
    onehot = jnp.arange(slot_count, dtype=jnp.int32)[:, None] == target[None, :]
    packed = jnp.dot(
        onehot.astype(jnp.float32),
        grad_events,
        precision=lax.Precision.HIGHEST,
        preferred_element_type=jnp.float32,
    )
    labels = jnp.sum(jnp.where(onehot, table_rows[None, :] + 1, 0), axis=1) - 1
    return (
        packed.reshape(data_size, loop_size, capacity, model_width),
        labels.reshape(data_size, loop_size, capacity),
    )


def merge_rows(received, row_marks):
    model_width = received.shape[-1]
    flat_rows = received.reshape(-1, model_width)
    flat_marks = row_marks.reshape(-1)
    matches = ((flat_marks[:, None] == flat_marks[None, :]) & (flat_marks[None, :] >= 0)).astype(
        jnp.float32
    )
    return jnp.dot(
        matches, flat_rows, precision=lax.Precision.HIGHEST, preferred_element_type=jnp.float32
    )


def body(
    events,
    out_grad,
    proj_weight,
    out_weight,
    lengths,
    tile_mask,
    quotient_shard,
    quotient_row,
    remainder_shard,
    remainder_row,
):
    row_count, model_width = events.shape
    loop_size = lax.axis_size("ctx")
    data_size = lax.axis_size("dp")
    loop_place = lax.axis_index("ctx")
    longest = float(row_count * loop_size // 2)
    score_scale = 1.0 / math.sqrt(model_width // HEADS)
    history = lengths[0]
    row_start = loop_place * row_count
    projected = jnp.dot(events, proj_weight, preferred_element_type=jnp.float32)
    sigmoid_proj = jax.nn.sigmoid(projected)
    activated = (projected * sigmoid_proj).astype(jnp.bfloat16)
    gate_rows = activated[:, :model_width].astype(jnp.float32)
    value_rows = activated[:, model_width : 2 * model_width]
    query_rows = activated[:, 2 * model_width : 3 * model_width]
    key_rows = activated[:, 3 * model_width :]
    query_heads = query_rows.reshape(row_count, HEADS, -1)
    empty_rows = jnp.zeros((row_count, model_width), jnp.float32)

    def forward_turn(turn_index, state):
        running, key_block, value_block = state
        offset_row = (loop_place - turn_index) % loop_size * row_count
        weight = visible_weight(
            history, tile_mask, row_start, row_count, offset_row, row_count, longest
        )
        running = running + guarded(
            weight,
            lambda: forward_block(query_heads, key_block, value_block, weight, score_scale),
            empty_rows,
        )
        key_next, value_next = passed_along((key_block, value_block), "ctx", 1)
        return (running, key_next, value_next)

    mixed_rows, key_spent, value_spent = lax.fori_loop(
        0, loop_size, forward_turn, (empty_rows, key_rows, value_rows)
    )
    row_mean = jnp.mean(mixed_rows, axis=1, keepdims=True)
    centered = mixed_rows - row_mean
    inv_scale = lax.rsqrt(jnp.mean(centered * centered, axis=1, keepdims=True) + EPSILON)
    normed = centered * inv_scale
    gated_rows = (normed * gate_rows).astype(jnp.bfloat16)
    out_weight_term = jnp.einsum(
        "td,te->de", gated_rows, out_grad, preferred_element_type=jnp.float32
    )
    grad_gated = jnp.einsum("te,de->td", out_grad, out_weight, preferred_element_type=jnp.float32)
    grad_normed = grad_gated * gate_rows
    grad_gate = grad_gated * normed
    grad_mixed = (
        inv_scale
        * (
            grad_normed
            - jnp.mean(grad_normed, axis=1, keepdims=True)
            - normed * jnp.mean(grad_normed * normed, axis=1, keepdims=True)
        )
    ).astype(jnp.bfloat16)
    grad_heads = grad_mixed.reshape(row_count, HEADS, -1)
    empty_triple = (empty_rows, empty_rows, empty_rows)

    def cycle_turn(turn_index, state):
        grad_query, key_block, value_block, key_grad_block, value_grad_block = state
        offset_row = (loop_place - turn_index) % loop_size * row_count
        weight = visible_weight(
            history, tile_mask, row_start, row_count, offset_row, row_count, longest
        )
        query_add, key_add, value_add = guarded(
            weight,
            lambda: backward_block(
                query_heads, grad_heads, key_block, value_block, weight, score_scale
            ),
            empty_triple,
        )
        key_next, value_next = passed_along((key_block, value_block), "ctx", 1)
        key_grad_next, value_grad_next = from_behind(
            (key_grad_block + key_add, value_grad_block + value_add), "ctx", 1
        )
        return (grad_query + query_add, key_next, value_next, key_grad_next, value_grad_next)

    grad_query, key_back, value_back, grad_keys, grad_values = lax.fori_loop(
        0, loop_size, cycle_turn, (empty_rows, key_rows, value_rows, empty_rows, empty_rows)
    )
    grad_projected = (
        jnp.concatenate([grad_gate, grad_values, grad_query, grad_keys], axis=1)
        * silu_grad(projected, sigmoid_proj)
    ).astype(jnp.bfloat16)
    grad_events = out_grad.astype(jnp.float32) + jnp.einsum(
        "tf,df->td", grad_projected, proj_weight, preferred_element_type=jnp.float32
    )
    proj_weight_term = jnp.einsum(
        "td,tf->df", events, grad_projected, preferred_element_type=jnp.float32
    )
    proj_weight_grad, out_weight_grad = lax.psum((proj_weight_term, out_weight_term), ("dp", "ctx"))
    devices = data_size * loop_size
    capacity = max(2, 3 * row_count // (2 * devices))
    quotient_buffer, quotient_labels = pack_rows(
        grad_events, quotient_shard, quotient_row, data_size, loop_size, capacity
    )
    remainder_buffer, remainder_labels = pack_rows(
        grad_events, remainder_shard, remainder_row, data_size, loop_size, capacity
    )
    quotient_in, remainder_in, quotient_marks, remainder_marks = (
        lax.all_to_all(
            lax.all_to_all(quotient_buffer, "dp", split_axis=0, concat_axis=0, tiled=True),
            "ctx",
            split_axis=1,
            concat_axis=1,
            tiled=True,
        ),
        lax.all_to_all(
            lax.all_to_all(remainder_buffer, "dp", split_axis=0, concat_axis=0, tiled=True),
            "ctx",
            split_axis=1,
            concat_axis=1,
            tiled=True,
        ),
        lax.all_to_all(
            lax.all_to_all(quotient_labels, "dp", split_axis=0, concat_axis=0, tiled=True),
            "ctx",
            split_axis=1,
            concat_axis=1,
            tiled=True,
        ),
        lax.all_to_all(
            lax.all_to_all(remainder_labels, "dp", split_axis=0, concat_axis=0, tiled=True),
            "ctx",
            split_axis=1,
            concat_axis=1,
            tiled=True,
        ),
    )
    quotient_grads = merge_rows(quotient_in, quotient_marks)
    remainder_grads = merge_rows(remainder_in, remainder_marks)
    return (quotient_grads, remainder_grads, proj_weight_grad, out_weight_grad)


def solution(mesh):
    in_specs = (
        P(("dp", "ctx"), None),
        P(("dp", "ctx"), None),
        P(),
        P(),
        P("dp", None),
        P("dp", None),
        P(("dp", "ctx")),
        P(("dp", "ctx")),
        P(("dp", "ctx")),
        P(("dp", "ctx")),
    )
    out_specs = (P(("dp", "ctx"), None), P(("dp", "ctx"), None), P(), P())
    return jax.shard_map(body, mesh=mesh, in_specs=in_specs, out_specs=out_specs, check_vma=False)
```

profile of v0, /device:TPU:0, one launch (start us, length us, event | category | flops | bytes accessed | tf_op | source)
XLA Modules:
  0.0 401.7 jit_solution(2794665894758102020)
XLA Ops:
  9.8 7.4 %all-to-all-start.4 = ((s32[16,2,12]{2,1,0:T(2,128)}), s32[16,2,12]{2,1,0:T(2,128)S(1)}, u32[]{:S(2)}, u32[]{:S(2)}) async-start(s32[16,2,12]{2,1,0:T(2,128)} %sub.96), calls=%async_computation.4 | async-start | bytes 32768 | tf_op jit(solution)/shard_map/all_to_all | solution.py:269
  17.2 3.0 multiply_convert_fusion.4
  26.6 32.6 %while.46 = (s32[]{:T(128)}, f32[256,512]{0,1:T(8,128)S(1)}, bf16[256,512]{0,1:T(8,128)(2,1)S(1)}, bf16[256,512]{0,1:T(8,128)(2,1)}, s32[]{:T(128)}, /*index=5*/...) while((s32[]{:T(128)}, f32[256,512]{0,1:T(8,128)S(1)}, ...), condition=%wide.region_9.10_spmd.clone, body=%wide.region_3.9_spmd.clone.sunk | while | flops 141884944 | bytes 6576610 | solution.py:180
  27.3 3.4 collective-permute-start
  39.6 3.2 collective-permute-done.1
  43.5 4.4 %collective-permute-start = (bf16[256,512]{0,1:T(8,128)(2,1)}, bf16[256,512]{0,1:T(8,128)(2,1)S(1)}, u32[]{:S(2)}, u32[]{:S(2)}) collective-permute-start(bf16[256,512]{0,1:T(8,128)(2,1)} %copy.97), channel_id=1, source_target_pairs={{0,1},{2,3},{4,5},{6,7},{8,9},{10,11},{12,13},{14,15},{16,17},{18,... | collective-permute-start | bytes 786440 | tf_op jit(solution)/shard_map/while/body/eval_jaxpr/ppermute | solution.py:18
  54.9 4.2 %collective-permute-done.1 = bf16[256,512]{0,1:T(8,128)(2,1)} collective-permute-done((bf16[256,512]{0,1:T(8,128)(2,1)}, bf16[256,512]{0,1:T(8,128)(2,1)}, u32[]{:S(2)}, u32[]{:S(2)}) %collective-permute-start.1) | collective-permute-done | bytes 262176 | tf_op jit(solution)/shard_map/while/body/eval_jaxpr/ppermute | solution.py:18
  66.6 90.7 %while.47 = (s32[]{:T(128)}, f32[256,512]{0,1:T(8,128)}, bf16[256,512]{0,1:T(8,128)(2,1)}, bf16[256,512]{0,1:T(8,128)(2,1)}, f32[256,512]{0,1:T(8,128)}, /*index...) while((s32[]{:T(128)}, f32[256,512]{0,1:T(8,128)}, ...), condition=%wide.region_20.21_spmd.clone, body=%wide.region_14.0_spmd.clone.sunk | while | flops 349502976 | bytes 29907636 | solution.py:224
  71.9 6.0 %conditional.7 = (f32[256,512]{0,1:T(8,128)S(1)}, f32[256,512]{0,1:T(8,128)S(1)}, f32[256,512]{0,1:T(8,128)S(1)}) conditional(s32[]{:T(128)} %convert_element_type.188, () %tuple.154, (bf16[256,512]{0,1:T(8,128)(2,1)}, bf16[256,8,64]{0,2,1:T(8,128)(2,1)}, f32[256,256]{1,0:T(8,128)}, bf16[256,512]{0,1:T(8,128)(2,1)S(1)}, ...), branch_computations={%region_18.18_spmd, %region_19.19_spmd} | conditional | flops 345243648 | bytes 15466576 | solution.py:50
  83.7 4.6 %collective-permute-start.2 = (bf16[256,512]{0,1:T(8,128)(2,1)S(1)}, bf16[256,512]{0,1:T(8,128)(2,1)}, u32[]{:S(2)}, u32[]{:S(2)}) collective-permute-start(bf16[256,512]{0,1:T(8,128)(2,1)S(1)} %copy.111), channel_id=1, source_target_pairs={{0,1},{2,3},{4,5},{6,7},{8,9},{10,11},{12,13},{14,15},{16,17},{18,... | collective-permute-start | bytes 786440 | tf_op jit(solution)/shard_map/while/body/eval_jaxpr/ppermute | solution.py:18
  92.2 19.7 %collective-permute-done.2 = bf16[256,512]{0,1:T(8,128)(2,1)} collective-permute-done((bf16[256,512]{0,1:T(8,128)(2,1)S(1)}, bf16[256,512]{0,1:T(8,128)(2,1)}, u32[]{:S(2)}, u32[]{:S(2)}) %collective-permute-start.2) | collective-permute-done | bytes 262176 | tf_op jit(solution)/shard_map/while/body/eval_jaxpr/ppermute | solution.py:18
  111.9 3.4 collective-permute-done.3
  126.6 4.6 %collective-permute-start.2 = (bf16[256,512]{0,1:T(8,128)(2,1)S(1)}, bf16[256,512]{0,1:T(8,128)(2,1)}, u32[]{:S(2)}, u32[]{:S(2)}) collective-permute-start(bf16[256,512]{0,1:T(8,128)(2,1)S(1)} %copy.111), channel_id=1, source_target_pairs={{0,1},{2,3},{4,5},{6,7},{8,9},{10,11},{12,13},{14,15},{16,17},{18,... | collective-permute-start | bytes 786440 | tf_op jit(solution)/shard_map/while/body/eval_jaxpr/ppermute | solution.py:18
  135.3 19.2 %collective-permute-done.2 = bf16[256,512]{0,1:T(8,128)(2,1)} collective-permute-done((bf16[256,512]{0,1:T(8,128)(2,1)S(1)}, bf16[256,512]{0,1:T(8,128)(2,1)}, u32[]{:S(2)}, u32[]{:S(2)}) %collective-permute-start.2) | collective-permute-done | bytes 262176 | tf_op jit(solution)/shard_map/while/body/eval_jaxpr/ppermute | solution.py:18
  154.4 2.9 collective-permute-done.3
  164.2 9.7 %all-to-all-start = ((s32[16,2,12]{2,1,0:T(2,128)}), s32[16,2,12]{2,1,0:T(2,128)S(1)}, u32[]{:S(2)}, u32[]{:S(2)}) async-start(s32[16,2,12]{2,1,0:T(2,128)} %sub.88), calls=%async_computation | async-start | bytes 32768 | tf_op jit(solution)/shard_map/all_to_all | solution.py:262
  173.9 3.0 fusion.19
  180.4 3.7 all-to-all-start.5
  187.9 3.3 all-to-all-start.1
  195.9 2.8 copy.75
  198.7 4.3 %all-to-all-start.6 = ((f32[16,2,12,512]{3,1,2,0:T(2,128)}), f32[16,2,12,512]{3,1,2,0:T(2,128)}, u32[]{:S(2)}, u32[]{:S(2)}) async-start(f32[16,2,12,512]{3,1,2,0:T(2,128)} %copy.75), calls=%async_computation.6 | async-start | bytes 1572864 | tf_op jit(solution)/shard_map/all_to_all | solution.py:255
  207.2 2.8 convolution_bitcast_fusion
  209.9 11.7 %all-to-all-done.6 = f32[16,2,12,512]{3,1,2,0:T(2,128)} async-done(((f32[16,2,12,512]{3,1,2,0:T(2,128)}), f32[16,2,12,512]{3,1,2,0:T(2,128)}, u32[]{:S(2)}, u32[]{:S(2)}) %all-to-all-start.6) | async-done | bytes 786464 | tf_op jit(solution)/shard_map/all_to_all | solution.py:255
  221.7 5.4 %all-to-all-start.2 = ((f32[16,2,12,512]{3,1,2,0:T(2,128)}), f32[16,2,12,512]{3,1,2,0:T(2,128)S(1)}, u32[]{:S(2)}, u32[]{:S(2)}) async-start(f32[16,2,12,512]{3,1,2,0:T(2,128)} %copy.70), calls=%async_computation.2 | async-start | bytes 1572864 | tf_op jit(solution)/shard_map/all_to_all | solution.py:248
  232.1 13.8 %all-to-all-done.2 = f32[16,2,12,512]{3,1,2,0:T(2,128)S(1)} async-done(((f32[16,2,12,512]{3,1,2,0:T(2,128)}), f32[16,2,12,512]{3,1,2,0:T(2,128)S(1)}, u32[]{:S(2)}, u32[]{:S(2)}) %all-to-all-start.2) | async-done | bytes 786464 | tf_op jit(solution)/shard_map/all_to_all | solution.py:248
  246.8 3.5 all-to-all-start.7
  255.2 10.7 %all-to-all-done.7 = f32[16,2,12,512]{3,0,2,1:T(8,128)S(1)} async-done(((f32[16,2,12,512]{3,0,2,1:T(8,128)}), f32[16,2,12,512]{3,0,2,1:T(8,128)S(1)}, u32[]{:S(2)}, u32[]{:S(2)}) %all-to-all-start.7) | async-done | bytes 786464 | tf_op jit(solution)/shard_map/all_to_all | solution.py:254
  265.9 4.3 %all-to-all-start.3 = ((f32[16,2,12,512]{3,0,2,1:T(8,128)}), f32[16,2,12,512]{3,0,2,1:T(8,128)}, u32[]{:S(2)}, u32[]{:S(2)}) async-start(f32[16,2,12,512]{3,0,2,1:T(8,128)} %copy.71), calls=%async_computation.3 | async-start | bytes 1572864 | tf_op jit(solution)/shard_map/all_to_all | solution.py:247
  272.9 8.6 %all-to-all-done.3 = f32[16,2,12,512]{3,0,2,1:T(8,128)} async-done(((f32[16,2,12,512]{3,0,2,1:T(8,128)}), f32[16,2,12,512]{3,0,2,1:T(8,128)}, u32[]{:S(2)}, u32[]{:S(2)}) %all-to-all-start.3) | async-done | bytes 786464 | tf_op jit(solution)/shard_map/all_to_all | solution.py:247
  284.0 3.0 fusion.20
  288.7 99.8 %all-reduce.3.cloned.1.call-done = (f32[512,2048]{0,1:T(8,128)}, f32[512,512]{1,0:T(8,128)}) async-done(((f32[512,2048]{0,1:T(8,128)}, f32[512,512]{1,0:T(8,128)}), (f32[512,2048]{0,1:T(8,128)}, f32[512,512]{1,0:T(8,128)})) %all-reduce.3.cloned.1.call-update) | async-done | bytes 5242896 | tf_op jit(solution)/shard_map/psum | solution.py:237
  388.5 5.4 %copy.78 = f32[512,2048]{1,0:T(8,128)} copy(f32[512,2048]{0,1:T(8,128)} %get-tuple-element.865) | data formatting | bytes 8388608
  (177 shorter events, 111.2 us)
Async XLA Ops:
  7.2 10.0 %copy-start = (bf16[512,2048]{1,0:T(8,128)(2,1)S(1)}, bf16[512,2048]{1,0:T(8,128)(2,1)}, u32[]{:S(2)}) copy-start(bf16[512,2048]{1,0:T(8,128)(2,1)} %param.20) | copy-start | bytes 6291460
  9.8 154.4 %all-to-all-start.4 = ((s32[16,2,12]{2,1,0:T(2,128)}), s32[16,2,12]{2,1,0:T(2,128)S(1)}, u32[]{:S(2)}, u32[]{:S(2)}) async-start(s32[16,2,12]{2,1,0:T(2,128)} %sub.96), calls=%async_computation.4 | async-start | bytes 32768 | tf_op jit(solution)/shard_map/all_to_all | solution.py:269
  21.2 5.2 %copy-start.17 = (s32[4,4]{1,0:T(4,128)S(1)}, s32[4,4]{1,0:T(4,128)}, u32[]{:S(2)}) copy-start(s32[4,4]{1,0:T(4,128)} %param.23) | copy-start | bytes 196
  21.2 5.2 %copy-start.19 = (s32[1,4]{1,0:T(1,128)S(1)}, s32[1,4]{1,0:T(1,128)}, u32[]{:S(2)}) copy-start(s32[1,4]{1,0:T(1,128)} %param.22) | copy-start | bytes 52
  27.3 12.2 %collective-permute-start = (bf16[256,512]{0,1:T(8,128)(2,1)}, bf16[256,512]{0,1:T(8,128)(2,1)S(1)}, u32[]{:S(2)}, u32[]{:S(2)}) collective-permute-start(bf16[256,512]{0,1:T(8,128)(2,1)} %copy.97), channel_id=1, source_target_pairs={{0,1},{2,3},{4,5},{6,7},{8,9},{10,11},{12,13},{14,15},{16,17},{18,... | collective-permute-start | bytes 786440 | tf_op jit(solution)/shard_map/while/body/eval_jaxpr/ppermute | solution.py:18
  32.4 10.4 %collective-permute-start.1 = (bf16[256,512]{0,1:T(8,128)(2,1)}, bf16[256,512]{0,1:T(8,128)(2,1)}, u32[]{:S(2)}, u32[]{:S(2)}) collective-permute-start(bf16[256,512]{0,1:T(8,128)(2,1)} %copy.98), channel_id=1, source_target_pairs={{0,1},{2,3},{4,5},{6,7},{8,9},{10,11},{12,13},{14,15},{16,17},{18,... | collective-permute-start | bytes 786440 | tf_op jit(solution)/shard_map/while/body/eval_jaxpr/ppermute | solution.py:18
  43.5 11.4 %collective-permute-start = (bf16[256,512]{0,1:T(8,128)(2,1)}, bf16[256,512]{0,1:T(8,128)(2,1)S(1)}, u32[]{:S(2)}, u32[]{:S(2)}) collective-permute-start(bf16[256,512]{0,1:T(8,128)(2,1)} %copy.97), channel_id=1, source_target_pairs={{0,1},{2,3},{4,5},{6,7},{8,9},{10,11},{12,13},{14,15},{16,17},{18,... | collective-permute-start | bytes 786440 | tf_op jit(solution)/shard_map/while/body/eval_jaxpr/ppermute | solution.py:18
  49.6 9.6 %collective-permute-start.1 = (bf16[256,512]{0,1:T(8,128)(2,1)}, bf16[256,512]{0,1:T(8,128)(2,1)}, u32[]{:S(2)}, u32[]{:S(2)}) collective-permute-start(bf16[256,512]{0,1:T(8,128)(2,1)} %copy.98), channel_id=1, source_target_pairs={{0,1},{2,3},{4,5},{6,7},{8,9},{10,11},{12,13},{14,15},{16,17},{18,... | collective-permute-start | bytes 786440 | tf_op jit(solution)/shard_map/while/body/eval_jaxpr/ppermute | solution.py:18
  60.1 4.6 %copy-start.18 = (s32[256]{0:T(256)S(1)}, s32[256]{0:T(256)}, u32[]{:S(2)}) copy-start(s32[256]{0:T(256)} %param.25) | copy-start | bytes 3076
  77.9 10.4 %copy-start.1 = (f32[256,512]{0,1:T(8,128)}, f32[256,512]{0,1:T(8,128)S(1)}, u32[]{:S(2)}) copy-start(f32[256,512]{0,1:T(8,128)S(1)} %get-tuple-element.1056) | copy-start | bytes 1572868 | tf_op jit(solution)/shard_map/while
  80.0 35.4 %collective-permute-start.4 = (f32[256,512]{0,1:T(8,128)}, f32[256,512]{0,1:T(8,128)}, u32[]{:S(2)}, u32[]{:S(2)}) collective-permute-start(f32[256,512]{0,1:T(8,128)} %add.446), channel_id=1, source_target_pairs={{0,1},{1,0},{2,3},{3,2},{4,5},{5,4},{6,7},{7,6},{8,9},{9,8},{10,11... | collective-permute-start | bytes 1572872 | tf_op jit(solution)/shard_map/while/body/eval_jaxpr/ppermute | solution.py:23
  83.6 31.8 %collective-permute-start.5 = (f32[256,512]{0,1:T(8,128)S(1)}, f32[256,512]{0,1:T(8,128)}, u32[]{:S(2)}, u32[]{:S(2)}) collective-permute-start(f32[256,512]{0,1:T(8,128)S(1)} %add.447), channel_id=1, source_target_pairs={{0,1},{1,0},{2,3},{3,2},{4,5},{5,4},{6,7},{7,6},{8,9},{9,8},{10,11... | collective-permute-start | bytes 1572872 | tf_op jit(solution)/shard_map/while/body/eval_jaxpr/ppermute | solution.py:23
  83.7 28.3 %collective-permute-start.2 = (bf16[256,512]{0,1:T(8,128)(2,1)S(1)}, bf16[256,512]{0,1:T(8,128)(2,1)}, u32[]{:S(2)}, u32[]{:S(2)}) collective-permute-start(bf16[256,512]{0,1:T(8,128)(2,1)S(1)} %copy.111), channel_id=1, source_target_pairs={{0,1},{2,3},{4,5},{6,7},{8,9},{10,11},{12,13},{14,15},{16,17},{18,... | collective-permute-start | bytes 786440 | tf_op jit(solution)/shard_map/while/body/eval_jaxpr/ppermute | solution.py:18
  88.3 27.1 %collective-permute-start.3 = (bf16[256,512]{0,1:T(8,128)(2,1)}, bf16[256,512]{0,1:T(8,128)(2,1)}, u32[]{:S(2)}, u32[]{:S(2)}) collective-permute-start(bf16[256,512]{0,1:T(8,128)(2,1)} %copy.112), channel_id=1, source_target_pairs={{0,1},{2,3},{4,5},{6,7},{8,9},{10,11},{12,13},{14,15},{16,17},{18,... | collective-permute-start | bytes 786440 | tf_op jit(solution)/shard_map/while/body/eval_jaxpr/ppermute | solution.py:18
  120.8 10.4 %copy-start.1 = (f32[256,512]{0,1:T(8,128)}, f32[256,512]{0,1:T(8,128)S(1)}, u32[]{:S(2)}) copy-start(f32[256,512]{0,1:T(8,128)S(1)} %get-tuple-element.1056) | copy-start | bytes 1572868 | tf_op jit(solution)/shard_map/while
  122.9 34.4 %collective-permute-start.4 = (f32[256,512]{0,1:T(8,128)}, f32[256,512]{0,1:T(8,128)}, u32[]{:S(2)}, u32[]{:S(2)}) collective-permute-start(f32[256,512]{0,1:T(8,128)} %add.446), channel_id=1, source_target_pairs={{0,1},{1,0},{2,3},{3,2},{4,5},{5,4},{6,7},{7,6},{8,9},{9,8},{10,11... | collective-permute-start | bytes 1572872 | tf_op jit(solution)/shard_map/while/body/eval_jaxpr/ppermute | solution.py:23
  126.5 30.9 %collective-permute-start.5 = (f32[256,512]{0,1:T(8,128)S(1)}, f32[256,512]{0,1:T(8,128)}, u32[]{:S(2)}, u32[]{:S(2)}) collective-permute-start(f32[256,512]{0,1:T(8,128)S(1)} %add.447), channel_id=1, source_target_pairs={{0,1},{1,0},{2,3},{3,2},{4,5},{5,4},{6,7},{7,6},{8,9},{9,8},{10,11... | collective-permute-start | bytes 1572872 | tf_op jit(solution)/shard_map/while/body/eval_jaxpr/ppermute | solution.py:23
  126.6 27.9 %collective-permute-start.2 = (bf16[256,512]{0,1:T(8,128)(2,1)S(1)}, bf16[256,512]{0,1:T(8,128)(2,1)}, u32[]{:S(2)}, u32[]{:S(2)}) collective-permute-start(bf16[256,512]{0,1:T(8,128)(2,1)S(1)} %copy.111), channel_id=1, source_target_pairs={{0,1},{2,3},{4,5},{6,7},{8,9},{10,11},{12,13},{14,15},{16,17},{18,... | collective-permute-start | bytes 786440 | tf_op jit(solution)/shard_map/while/body/eval_jaxpr/ppermute | solution.py:18
  131.2 26.1 %collective-permute-start.3 = (bf16[256,512]{0,1:T(8,128)(2,1)}, bf16[256,512]{0,1:T(8,128)(2,1)}, u32[]{:S(2)}, u32[]{:S(2)}) collective-permute-start(bf16[256,512]{0,1:T(8,128)(2,1)} %copy.112), channel_id=1, source_target_pairs={{0,1},{2,3},{4,5},{6,7},{8,9},{10,11},{12,13},{14,15},{16,17},{18,... | collective-permute-start | bytes 786440 | tf_op jit(solution)/shard_map/while/body/eval_jaxpr/ppermute | solution.py:18
  164.2 16.2 %all-to-all-start = ((s32[16,2,12]{2,1,0:T(2,128)}), s32[16,2,12]{2,1,0:T(2,128)S(1)}, u32[]{:S(2)}, u32[]{:S(2)}) async-start(s32[16,2,12]{2,1,0:T(2,128)} %sub.88), calls=%async_computation | async-start | bytes 32768 | tf_op jit(solution)/shard_map/all_to_all | solution.py:262
  173.9 10.2 %copy-start.13 = (bf16[256,512]{1,0:T(8,128)(2,1)S(1)}, bf16[256,512]{1,0:T(8,128)(2,1)}, u32[]{:S(2)}) copy-start(bf16[256,512]{1,0:T(8,128)(2,1)} %param.19) | copy-start | bytes 786436
  176.9 16.8 %copy-start.4 = (bf16[256,2048]{1,0:T(8,128)(2,1)}, bf16[256,2048]{1,0:T(8,128)(2,1)S(1)}, u32[]{:S(2)}) copy-start(bf16[256,2048]{1,0:T(8,128)(2,1)S(1)} %fusion.19) | copy-start | bytes 3145732
  180.4 7.5 %all-to-all-start.5 = ((s32[2,1,192]{2,1,0:T(1,128)}), s32[2,1,192]{2,1,0:T(1,128)S(1)}, u32[]{:S(2)}, u32[]{:S(2)}) async-start(s32[2,1,192]{2,1,0:T(1,128)} %reshape.303), calls=%async_computation.5 | async-start | bytes 4096 | tf_op jit(solution)/shard_map/all_to_all | solution.py:268
  187.9 10.8 %all-to-all-start.1 = ((s32[2,1,192]{2,1,0:T(1,128)}), s32[2,1,192]{2,1,0:T(1,128)S(1)}, u32[]{:S(2)}, u32[]{:S(2)}) async-start(s32[2,1,192]{2,1,0:T(1,128)} %reshape.301), calls=%async_computation.1 | async-start | bytes 4096 | tf_op jit(solution)/shard_map/all_to_all | solution.py:261
  195.9 7.1 %copy-start.10 = (f32[256,512]{1,0:T(8,128)S(1)}, f32[256,512]{1,0:T(8,128)}, u32[]{:S(2)}) copy-start(f32[256,512]{1,0:T(8,128)} %convolution_add_fusion) | copy-start | bytes 1572868
  198.7 23.0 %all-to-all-start.6 = ((f32[16,2,12,512]{3,1,2,0:T(2,128)}), f32[16,2,12,512]{3,1,2,0:T(2,128)}, u32[]{:S(2)}, u32[]{:S(2)}) async-start(f32[16,2,12,512]{3,1,2,0:T(2,128)} %copy.75), calls=%async_computation.6 | async-start | bytes 1572864 | tf_op jit(solution)/shard_map/all_to_all | solution.py:255
  207.2 20.0 %copy-start.3 = (f32[256,512]{1,0:T(8,128)S(1)}, f32[256,512]{1,0:T(8,128)}, u32[]{:S(2)}) copy-start(f32[256,512]{1,0:T(8,128)} %copy-done.2) | copy-start | bytes 1572868
  221.7 24.3 %all-to-all-start.2 = ((f32[16,2,12,512]{3,1,2,0:T(2,128)}), f32[16,2,12,512]{3,1,2,0:T(2,128)S(1)}, u32[]{:S(2)}, u32[]{:S(2)}) async-start(f32[16,2,12,512]{3,1,2,0:T(2,128)} %copy.70), calls=%async_computation.2 | async-start | bytes 1572864 | tf_op jit(solution)/shard_map/all_to_all | solution.py:248
  227.1 161.4 %all-reduce.3.cloned.1.call-start = ((), (), s32[]{:S(2)}) async-start(), calls=%async_computation.8 | async-start | bytes 10485760 | tf_op jit(solution)/shard_map/psum | solution.py:237
  246.8 19.0 %all-to-all-start.7 = ((f32[16,2,12,512]{3,0,2,1:T(8,128)}), f32[16,2,12,512]{3,0,2,1:T(8,128)S(1)}, u32[]{:S(2)}, u32[]{:S(2)}) async-start(f32[16,2,12,512]{3,0,2,1:T(8,128)} %copy.76), calls=%async_computation.7 | async-start | bytes 1572864 | tf_op jit(solution)/shard_map/all_to_all | solution.py:254
  265.9 15.5 %all-to-all-start.3 = ((f32[16,2,12,512]{3,0,2,1:T(8,128)}), f32[16,2,12,512]{3,0,2,1:T(8,128)}, u32[]{:S(2)}, u32[]{:S(2)}) async-start(f32[16,2,12,512]{3,0,2,1:T(8,128)} %copy.71), calls=%async_computation.3 | async-start | bytes 1572864 | tf_op jit(solution)/shard_map/all_to_all | solution.py:247
  388.5 5.4 %copy-start.11 = (f32[512,512]{1,0:T(8,128)S(1)}, f32[512,512]{1,0:T(8,128)}, u32[]{:S(2)}) copy-start(f32[512,512]{1,0:T(8,128)} %get-tuple-element.1155) | copy-start | bytes 3145732
  (11 other events, 26.2 us)
Sparse Core Ops, SparseCore 0:
  234.1 154.3 all-reduce.2
where the time goes:
time: 403 us; the launch traced here: 402 us
  waiting for transfers between devices  202 us (50%)
  starting transfers between devices  71.9 us (18%)
  local copies, waits for them, and re-layouts  54.6 us (14%)
  matrix products  36.2 us (9%)
  other arithmetic  20.1 us (5%)
  between operations  14.3 us (4%)
    psum x1, waiting for transfers between devices, body(): lax.psum((proj_weight_term, out_weight_term), ('dp', 'ctx'))  99.8 us
    ppermute x8, waiting for transfers between devices, passed_along(): return lax.ppermute(shard, axis, pairs)  53.2 us
    ppermute x8, starting transfers between devices, passed_along(): return lax.ppermute(shard, axis, pairs)  25 us
    unnamed x46, local copies, waits for them, and re-layouts  14.7 us
    all_to_all x1, waiting for transfers between devices, body(): lax.all_to_all(quotient_buffer, 'dp', split_axis=0, concat_axis=0, tiled=...  13.8 us
    all_to_all x1, waiting for transfers between devices, body(): lax.all_to_all(remainder_buffer, 'dp', split_axis=0, concat_axis=0, tiled...  11.7 us
    all_to_all x1, waiting for transfers between devices, body(): lax.all_to_all(lax.all_to_all(remainder_buffer, 'dp', split_axis=0, conca...  10.7 us
    while x12, local copies, waits for them, and re-layouts  10 us
  transfers between devices with their start and end apart: 21, of which 14 were waited for; matrix products, arithmetic and copies ran while one was open for 25% of the time, Pallas kernels for 0%

commit v1 on v0

--- a/solution.py
+++ b/solution.py
@@ -3,6 +3,8 @@
 import jax
 import jax.numpy as jnp
 from jax import lax
+from jax.experimental import pallas as pl
+from jax.experimental.pallas import tpu as pltpu
 from jax.sharding import PartitionSpec as P
 
 HEADS = 8
@@ -278,7 +280,404 @@
     return (quotient_grads, remainder_grads, proj_weight_grad, out_weight_grad)
 
 
+F32 = jnp.float32
+BF16 = jnp.bfloat16
+MESH = pl.DeviceIdType.MESH
+BLOCK = 32
+WIDTH = 512
+
+
+def dot_rows(a, b):
+    return lax.dot_general(a, b, (((1,), (1,)), ((), ())), preferred_element_type=F32)
+
+
+def dot_first(a, b):
+    return lax.dot_general(a, b, (((0,), (0,)), ((), ())), preferred_element_type=F32)
+
+
+def sigmoid_of(x):
+    return 0.5 * jnp.tanh(0.5 * x) + 0.5
+
+
+def layer_kernel(
+    place_ref, lengths_ref, tiles_ref, ev_own, og_own, ev_far, og_far, weight_ref, out_weight_ref,
+    shards_ref, rows_ref, pack_ref, wgrad_ref,
+    ev, og, act, dact, att, slope, mixed, gm, mask, gp, gated,
+):
+    half, width = ev_own.shape
+    full = 2 * half
+    place = place_ref[0]
+    own = pl.multiple_of(place * half, half)
+    far = pl.multiple_of((1 - place) * half, half)
+    ev[pl.ds(own, half), :] = ev_own[...]
+    ev[pl.ds(far, half), :] = ev_far[...]
+    og[pl.ds(own, half), :] = og_own[...]
+    og[pl.ds(far, half), :] = og_far[...]
+
+    ends = []
+    total = jnp.int32(0)
+    for k in range(lengths_ref.shape[1]):
+        total = total + lengths_ref[0, k]
+        ends.append(total)
+    longest = float(full // 2)
+    tiles = full // TILE
+    mask[...] = jnp.zeros_like(mask)
+    for a in range(tiles):
+        row = a * TILE + lax.broadcasted_iota(jnp.int32, (TILE, TILE), 0)
+        row_doc = sum((row >= e).astype(jnp.int32) for e in ends)
+        for b in range(a + 1):
+            col = b * TILE + lax.broadcasted_iota(jnp.int32, (TILE, TILE), 1)
+            col_doc = sum((col >= e).astype(jnp.int32) for e in ends)
+            keep = jnp.where(tiles_ref[a, b] == 1, 1.0 / longest, 0.0)
+            seen = (row_doc == col_doc) & (col <= row)
+            mask[a * TILE : (a + 1) * TILE, b * TILE : (b + 1) * TILE] = jnp.where(seen, keep, 0.0)
+
+    @pl.loop(0, 4 * width // 256)
+    def _(n):
+        cols = pl.ds(pl.multiple_of(n * 256, 256), 256)
+        projected = jnp.dot(ev[...], weight_ref[:, cols], preferred_element_type=F32)
+        sig = sigmoid_of(projected)
+        value = projected * sig
+        act[:, cols] = value.astype(BF16)
+        dact[:, cols] = sig * (1.0 + projected * (1.0 - sig))
+
+    scale = 1.0 / math.sqrt(width // HEADS)
+    head_width = width // HEADS
+    lane = lax.broadcasted_iota(jnp.int32, (1, 128), 1) // head_width
+
+    def pair_cols(base, p):
+        return pl.ds(pl.multiple_of(base * width + p * 128, 128), 128)
+
+    def only(x, h):
+        return jnp.where(lane == h, x, jnp.zeros_like(x))
+
+    blocks = ((0, half), (half, full))
+
+    @pl.loop(0, width // 128)
+    def _(p):
+        q = (act[:, pair_cols(2, p)].astype(F32) * scale).astype(BF16)
+        k = act[:, pair_cols(3, p)]
+        v = act[:, pair_cols(1, p)]
+        for lo, hi in blocks:
+            total = jnp.zeros((half, 128), F32)
+            for h in range(2):
+                scores = dot_rows(only(q[lo:hi], h), k[:hi])
+                sig = sigmoid_of(scores)
+                w = mask[lo:hi, :hi]
+                a = (scores * sig * w).astype(BF16)
+                att[p * 2 + h, lo:hi, :hi] = a
+                slope[p * 2 + h, lo:hi, :hi] = w * sig * (1.0 + scores * (1.0 - sig))
+                total = total + jnp.dot(a, only(v[:hi], h), preferred_element_type=F32)
+            mixed[lo:hi, pl.ds(pl.multiple_of(p * 128, 128), 128)] = total
+
+    @pl.loop(0, full // 128)
+    def _(r):
+        rows = pl.ds(pl.multiple_of(r * 128, 128), 128)
+        m = mixed[rows, :]
+        centered = m - jnp.mean(m, axis=1, keepdims=True)
+        inv = lax.rsqrt(jnp.mean(centered * centered, axis=1, keepdims=True) + EPSILON)
+        normed = centered * inv
+        gate = act[rows, :width].astype(F32)
+        gated[rows, :] = (normed * gate).astype(BF16)
+        grad_gated = dot_rows(og[rows, :], out_weight_ref[...])
+        grad_normed = grad_gated * gate
+        gp[rows, :width] = (grad_gated * normed * dact[rows, :width]).astype(BF16)
+        gm[rows, :] = (
+            inv
+            * (
+                grad_normed
+                - jnp.mean(grad_normed, axis=1, keepdims=True)
+                - normed * jnp.mean(grad_normed * normed, axis=1, keepdims=True)
+            )
+        ).astype(BF16)
+
+    @pl.loop(0, width // 128)
+    def _(p):
+        q = (act[:, pair_cols(2, p)].astype(F32) * scale).astype(BF16)
+        k = act[:, pair_cols(3, p)]
+        v = act[:, pair_cols(1, p)]
+        g = gm[:, pair_cols(0, p)]
+        dv = [jnp.zeros((half, 128), F32)] * 2
+        dk = [jnp.zeros((half, 128), F32)] * 2
+        dq = [jnp.zeros((half, 128), F32)] * 2
+        for h in range(2):
+            kh, gh, qh = only(k, h), only(g, h), only(q, h)
+            for n, (lo, hi) in enumerate(blocks):
+                grad_att = dot_rows(gh[lo:hi], v[:hi])
+                gs = (grad_att * slope[p * 2 + h, lo:hi, :hi]).astype(BF16)
+                dq[n] = dq[n] + jnp.dot(gs, kh[:hi], preferred_element_type=F32)
+                a = att[p * 2 + h, lo:hi, :hi]
+                for m in range(n + 1):
+                    at = slice(m * half, (m + 1) * half)
+                    dv[m] = dv[m] + dot_first(a[:, at], gh[lo:hi])
+                    dk[m] = dk[m] + dot_first(gs[:, at], qh[lo:hi])
+        for n, (lo, hi) in enumerate(blocks):
+            for base, value in ((1, dv[n]), (2, dq[n] * scale), (3, dk[n])):
+                cols = pair_cols(base, p)
+                gp[lo:hi, cols] = (value * dact[lo:hi, cols]).astype(BF16)
+
+    mine = pl.ds(own, half)
+    wgrad_ref[:, 4 * width :] = dot_first(gated[:, mine], og[...]).astype(BF16)
+    ev_mine = ev[:, mine]
+
+    @pl.loop(0, 4 * width // 512)
+    def _(n):
+        cols = pl.ds(pl.multiple_of(n * 512, 512), 512)
+        wgrad_ref[:, cols] = dot_first(ev_mine, gp[:, cols]).astype(BF16)
+
+    grad_events = (og_own[...].astype(F32) + dot_rows(gp[mine, :], weight_ref[...])).astype(BF16)
+
+    slots = pack_ref.shape[0]
+    capacity = 3 * half // (2 * (slots // BLOCK))
+    early = lax.broadcasted_iota(jnp.int32, (half, half), 0) < lax.broadcasted_iota(
+        jnp.int32, (half, half), 1
+    )
+    slot = lax.broadcasted_iota(jnp.int32, (slots, half), 0)
+    spot = lax.broadcasted_iota(jnp.int32, (128, half), 0)
+    onehot = jnp.zeros((slots, half), F32)
+    numbers = jnp.zeros((slots, 128), F32)
+    for t in range(2):
+        shard = shards_ref[t : t + 1, :]
+        across = jnp.broadcast_to(shard.astype(F32), (half, half))
+        same = (jnp.transpose(across) == across) & early
+        rank = jnp.sum(same.astype(F32), axis=0, keepdims=True).astype(jnp.int32)
+        at = rank + t * capacity
+        onehot = onehot + (slot == shard * BLOCK + at).astype(F32)
+        number = rows_ref[t : t + 1, :]
+        high = (number // 256 + 1).astype(F32)
+        low = (number % 256).astype(F32)
+        left = jnp.where(slot == shard * BLOCK + 2 * capacity, high, 0.0) + jnp.where(
+            slot == shard * BLOCK + 2 * capacity + 1, low, 0.0
+        )
+        numbers = numbers + dot_rows(left.astype(BF16), (spot == at).astype(BF16))
+    onehot = onehot.astype(BF16)
+    packed = jnp.dot(onehot, grad_events, preferred_element_type=F32)
+    pack_ref[:, :128] = (packed[:, :128] + numbers).astype(BF16)
+    pack_ref[:, 128:] = packed[:, 128:].astype(BF16)
+
+
+def exchange_kernel(
+    data_size, pack_ref, wgrad_ref, got_ref, sum_ref,
+    totals, outgo, income, local_sem, row_send, row_recv, red_send, red_recv, all_send, all_recv,
+):
+    data = lax.axis_index("dp")
+    place = lax.axis_index("ctx")
+    me = data * 2 + place
+    devices = data_size * 2
+    barrier = pltpu.get_barrier_semaphore()
+
+    def other(k):
+        to = lax.rem(me + k, devices)
+        return to, (to // 2, lax.rem(to, 2))
+
+    @pl.loop(1, devices)
+    def _(k):
+        _, where = other(k)
+        pl.semaphore_signal(barrier, inc=1, device_id=where, device_id_type=MESH)
+
+    pl.semaphore_wait(barrier, devices - 1)
+
+    steps = data_size.bit_length() - 1
+    height = wgrad_ref.shape[0]
+
+    def bit(n):
+        return lax.rem(data // (1 << n), 2)
+
+    def toward(n):
+        return (data + (1 - 2 * bit(n)) * (1 << n), place)
+
+    def remote(src, dst, send, recv, where):
+        return pltpu.make_async_remote_copy(
+            src_ref=src, dst_ref=dst, send_sem=send, recv_sem=recv, device_id=where,
+            device_id_type=MESH,
+        )
+
+    def reduce_copy(n):
+        size = height >> (n + 1)
+        if n == 0:
+            src = wgrad_ref.at[pl.ds(pl.multiple_of((1 - bit(0)) * size, size), size)]
+        else:
+            src = outgo.at[pl.ds(height - 2 * size, size)]
+        dst = income.at[pl.ds(height - 2 * size, size)]
+        return remote(src, dst, red_send.at[n], red_recv.at[n], toward(n))
+
+    first = reduce_copy(0)
+    first.start()
+
+    def row_copy(k):
+        to, where = other(k)
+        return remote(
+            pack_ref.at[pl.ds(pl.multiple_of(to * BLOCK, BLOCK), BLOCK)],
+            got_ref.at[pl.ds(pl.multiple_of(me * BLOCK, BLOCK), BLOCK)],
+            row_send.at[k],
+            row_recv.at[k],
+            where,
+        )
+
+    here = pl.ds(pl.multiple_of(me * BLOCK, BLOCK), BLOCK)
+    local = pltpu.make_async_copy(pack_ref.at[here], got_ref.at[here], local_sem)
+    local.start()
+
+    @pl.loop(1, devices)
+    def _(k):
+        row_copy(k).start()
+
+    offset = place * height
+    for n in range(steps):
+        size = height >> (n + 1)
+        came = pl.ds(height - 2 * size, size)
+        reduce_copy(n).wait_recv()
+        kept = pl.ds(pl.multiple_of(bit(n) * size, size), size)
+        if n == 0:
+            held = wgrad_ref[kept, :].astype(F32)
+        else:
+            held = totals[kept, :]
+        held = held + income[came, :].astype(F32)
+        offset = offset + bit(n) * size
+        if n + 1 < steps:
+            totals[:size, :] = held
+            part = size // 2
+            gone = pl.ds(pl.multiple_of((1 - bit(n + 1)) * part, part), part)
+            outgo[pl.ds(height - 2 * part, part), :] = totals[gone, :].astype(BF16)
+            reduce_copy(n + 1).start()
+        else:
+            sum_ref[pl.ds(pl.multiple_of(offset, size), size), :] = held.astype(BF16)
+
+    def spread(n, start, size, where):
+        rows = sum_ref.at[pl.ds(pl.multiple_of(start, size), size)]
+        return remote(rows, rows, all_send.at[n], all_recv.at[n], where)
+
+    size = height >> steps
+    sent = []
+    for n in range(steps - 1, 0, -1):
+        copy = spread(n, offset, size, toward(n))
+        copy.start()
+        sent.append(copy)
+        copy.wait_recv()
+        offset = offset - bit(n) * size
+        size = 2 * size
+    ctx_copy = spread(steps, offset, size, (data, 1 - place))
+    ctx_copy.start()
+    near = spread(0, offset, size, toward(0))
+    near.start()
+    ctx_copy.wait_recv()
+    back = spread(steps + 1, offset + (1 - 2 * place) * height, size, toward(0))
+    back.start()
+    near.wait_recv()
+    back.wait_recv()
+    for copy in sent + [ctx_copy, near, back]:
+        copy.wait_send()
+    for n in range(steps):
+        reduce_copy(n).wait_send()
+    local.wait()
+
+    @pl.loop(1, devices)
+    def _(k):
+        copy = row_copy(k)
+        copy.wait_send()
+        copy.wait_recv()
+
+
+def pair_body(
+    events, out_grad, proj_weight, out_weight, lengths, tile_mask,
+    quotient_shard, quotient_row, remainder_shard, remainder_row,
+):
+    half, width = events.shape
+    data_size = lax.axis_size("dp")
+    devices = 2 * data_size
+    capacity = 3 * half // (2 * devices)
+    full = 2 * half
+    swap = [(0, 1), (1, 0)]
+    ev_far = lax.ppermute(events, "ctx", swap)
+    og_far = lax.ppermute(out_grad, "ctx", swap)
+    place = lax.axis_index("ctx").astype(jnp.int32).reshape(1)
+    shards = jnp.stack([quotient_shard, remainder_shard])
+    numbers = jnp.stack([quotient_row, remainder_row])
+    vmem = pl.BlockSpec(memory_space=pltpu.VMEM)
+    smem = pl.BlockSpec(memory_space=pltpu.SMEM)
+    packed, wgrad = pl.pallas_call(
+        layer_kernel,
+        name="layer",
+        out_shape=(
+            jax.ShapeDtypeStruct((devices * BLOCK, width), BF16),
+            jax.ShapeDtypeStruct((half, 5 * width), BF16),
+        ),
+        in_specs=[smem] * 3 + [vmem] * 8,
+        out_specs=(vmem, vmem),
+        scratch_shapes=[
+            pltpu.VMEM((full, width), BF16),
+            pltpu.VMEM((full, width), BF16),
+            pltpu.VMEM((full, 4 * width), BF16),
+            pltpu.VMEM((full, 4 * width), F32),
+            pltpu.VMEM((HEADS, full, full), BF16),
+            pltpu.VMEM((HEADS, full, full), F32),
+            pltpu.VMEM((full, width), F32),
+            pltpu.VMEM((full, width), BF16),
+            pltpu.VMEM((full, full), F32),
+            pltpu.VMEM((full, 4 * width), BF16),
+            pltpu.VMEM((full, width), BF16),
+        ],
+        compiler_params=pltpu.CompilerParams(vmem_limit_bytes=56 * 2**20),
+        cost_estimate=pl.CostEstimate(
+            flops=10 * 10**9, bytes_accessed=8 * 2**20, transcendentals=4 * 10**6
+        ),
+    )(
+        place, lengths, tile_mask, events, out_grad, ev_far, og_far, proj_weight, out_weight,
+        shards, numbers,
+    )
+    steps = data_size.bit_length() - 1
+    got, sums = pl.pallas_call(
+        lambda *refs: exchange_kernel(data_size, *refs),
+        name="exchange",
+        out_shape=(
+            jax.ShapeDtypeStruct((devices * BLOCK, width), BF16),
+            jax.ShapeDtypeStruct((full, 5 * width), BF16),
+        ),
+        in_specs=[vmem, vmem],
+        out_specs=(vmem, vmem),
+        scratch_shapes=[
+            pltpu.VMEM((half // 2, 5 * width), F32),
+            pltpu.VMEM((half, 5 * width), BF16),
+            pltpu.VMEM((half, 5 * width), BF16),
+            pltpu.SemaphoreType.DMA,
+            pltpu.SemaphoreType.DMA((devices,)),
+            pltpu.SemaphoreType.DMA((devices,)),
+            pltpu.SemaphoreType.DMA((steps,)),
+            pltpu.SemaphoreType.DMA((steps,)),
+            pltpu.SemaphoreType.DMA((steps + 2,)),
+            pltpu.SemaphoreType.DMA((steps + 2,)),
+        ],
+        compiler_params=pltpu.CompilerParams(
+            collective_id=0, has_side_effects=True, vmem_limit_bytes=40 * 2**20
+        ),
+        cost_estimate=pl.CostEstimate(flops=10**6, bytes_accessed=8 * 2**20, transcendentals=0),
+    )(packed, wgrad)
+    blocks = got.reshape(devices, BLOCK, width)
+    head = blocks[:, 2 * capacity : 2 * capacity + 2, : 2 * capacity].astype(jnp.int32)
+    marks = jnp.where(head[:, 0] > 0, (head[:, 0] - 1) * 256 + head[:, 1], -1)
+    blank = jnp.full((devices, BLOCK), -1, jnp.int32)
+    grads = []
+    for t in range(2):
+        mine = marks[:, t * capacity : (t + 1) * capacity]
+        keys = lax.dynamic_update_slice(blank, mine, (0, t * capacity)).reshape(-1)
+        slots = mine.reshape(-1)
+        matches = (slots[:, None] == keys[None, :]) & (keys[None, :] >= 0)
+        grads.append(jnp.dot(matches.astype(BF16), got, preferred_element_type=F32))
+    return (
+        grads[0],
+        grads[1],
+        sums[:, : 4 * width].astype(F32),
+        sums[:, 4 * width :].astype(F32),
+    )
+
+
+def pair_fits(mesh):
+    data_size, loop_size = mesh.shape["dp"], mesh.shape["ctx"]
+    return loop_size == 2 and data_size == 16
+
+
 def solution(mesh):
+    chosen = pair_body if pair_fits(mesh) else body
     in_specs = (
         P(("dp", "ctx"), None),
         P(("dp", "ctx"), None),
@@ -292,4 +691,4 @@
         P(("dp", "ctx")),
     )
     out_specs = (P(("dp", "ctx"), None), P(("dp", "ctx"), None), P(), P())
-    return jax.shard_map(body, mesh=mesh, in_specs=in_specs, out_specs=out_specs, check_vma=False)
+    return jax.shard_map(chosen, mesh=mesh, in_specs=in_specs, out_specs=out_specs, check_vma=False)

time: 403 us -> 121 us (0.30)
  waiting for transfers between devices: 202 us -> 10.7 us
  Pallas kernels: 0 us -> 92.1 us
  starting transfers between devices: 71.9 us -> 3.08 us
  local copies, waits for them, and re-layouts: 54.6 us -> 4.74 us
  matrix products: 36.2 us -> 4.3 us
  other arithmetic: 20.1 us -> 5 us
  between operations: 14.3 us -> 0.69 us
    psum x1 -> x0, waiting for transfers between devices: 99.8 us -> none  [body(): lax.psum((proj_weight_term, out_weight_term), ('dp', 'ctx'))]
    pallas_call x0 -> x2, Pallas kernels: none -> 92.1 us  [the longest x1 70.9 us: pair_body(): pl.pallas_call(lambda *refs: exchange_kernel(data_size, *refs), name='exc...]
    all_to_all x8 -> x0, waiting for transfers between devices: 49 us -> none  [the longest x1 13.8 us: body(): lax.all_to_all(quotient_buffer, 'dp', split_axis=0, concat_axis=0, tiled=...]
    ppermute x12 -> x2, waiting for transfers between devices: 53.2 us -> 10.7 us  [the longest x1 5.95 us: pair_body(): ev_far = lax.ppermute(events, 'ctx', swap)]
    all_to_all x8 -> x0, starting transfers between devices: 41.7 us -> none  [the longest x1 9.67 us: body(): lax.all_to_all(quotient_labels, 'dp', split_axis=0, concat_axis=0, tiled=...]
    dot_general x23 -> x2, matrix products: 36.2 us -> 4.3 us  [pair_body(): grads.append(jnp.dot(matches.astype(BF16), got, preferred_element_type=F32))]
    ppermute x12 -> x2, starting transfers between devices: 30.1 us -> 3.08 us  [the longest x1 3 us: pair_body(): ev_far = lax.ppermute(events, 'ctx', swap)]
    while x16 -> x0, local copies, waits for them, and re-layouts: 16.3 us -> none
  transfers between devices with their start and end apart: 21 -> 2, of which waited for: 14 -> 2; matrix products, arithmetic and copies ran while one was open for 25% -> 1% of each run, Pallas kernels for 0% -> 0%
where the time goes in v1:
time: 121 us
  Pallas kernels  92.1 us (76%)
  waiting for transfers between devices  10.7 us (9%)
  other arithmetic  5 us (4%)
  local copies, waits for them, and re-layouts  4.74 us (4%)
  matrix products  4.3 us (4%)
  starting transfers between devices  3.08 us (3%)
    pallas_call x1, Pallas kernels, pair_body(): pl.pallas_call(lambda *refs: exchange_kernel(data_size, *refs), name='exc...  70.9 us
    pallas_call x1, Pallas kernels, pair_body(): pl.pallas_call(layer_kernel, name='layer', out_shape=(jax.ShapeDtypeStruc...  21.3 us
    ppermute x1, waiting for transfers between devices, pair_body(): ev_far = lax.ppermute(events, 'ctx', swap)  5.95 us
    ppermute x1, waiting for transfers between devices, pair_body(): og_far = lax.ppermute(out_grad, 'ctx', swap)  4.79 us
    dot_general x2, matrix products, pair_body(): grads.append(jnp.dot(matches.astype(BF16), got, preferred_element_type=F32))  4.3 us
    unnamed x12, local copies, waits for them, and re-layouts  4.21 us
    ppermute x1, starting transfers between devices, pair_body(): ev_far = lax.ppermute(events, 'ctx', swap)  3 us
    convert_element_type x1, other arithmetic, pair_body(): sums[:, :4 * width].astype(F32)  2.56 us
  transfers between devices with their start and end apart: 2, of which 2 were waited for; matrix products, arithmetic and copies ran while one was open for 1% of the time, Pallas kernels for 0%

profile of v1, /device:TPU:0, one launch (start us, length us, event | category | flops | bytes accessed | tf_op | source)
XLA Modules:
  0.0 120.7 jit_solution(15653474380778591277)
XLA Ops:
  0.6 3.0 %collective-permute-start = (bf16[256,512]{1,0:T(8,128)(2,1)}, bf16[256,512]{1,0:T(8,128)(2,1)S(1)}, u32[]{:S(2)}, u32[]{:S(2)}) collective-permute-start(bf16[256,512]{1,0:T(8,128)(2,1)} %ev_own.1), channel_id=1, source_target_pairs={{0,1},{1,0},{2,3},{3,2},{4,5},{5,4},{6,7},{7,6},{8,9},{9,8},{10,11... | collective-permute-start | bytes 786440 | tf_op jit(solution)/shard_map/ppermute | solution.py:591
  3.6 0.1 collective-permute-start.1
  3.7 1.3 %pad_add_fusion = (s32[2,256]{1,0:T(2,128)}, s32[2,256]{1,0:T(2,128)}) fusion(s32[1,256]{1,0:T(1,128)} %bitcast.11, s32[1,256]{1,0:T(1,128)} %bitcast.12, s32[1,256]{1,0:T(1,128)} %bitcast.13, s32[1,256]{1,0:T(1,128)} %bitcast.14), kind=kLoop, calls=%fused_computation.18 | loop fusion | flops 1024 | bytes 8192 | tf_op jit(solution)/shard_map/stack | solution.py:594
  5.0 6.0 %collective-permute-done.ev_far = bf16[256,512]{1,0:T(8,128)(2,1)S(1)} collective-permute-done((bf16[256,512]{1,0:T(8,128)(2,1)}, bf16[256,512]{1,0:T(8,128)(2,1)S(1)}, u32[]{:S(2)}, u32[]{:S(2)}) %collective-permute-start) | collective-permute-done | bytes 262176 | tf_op jit(solution)/shard_map/ppermute | solution.py:591
  11.0 0.0 copy-start.4
  11.0 4.8 %collective-permute-done.1.og_far = bf16[256,512]{1,0:T(8,128)(2,1)S(1)} collective-permute-done((bf16[256,512]{1,0:T(8,128)(2,1)}, bf16[256,512]{1,0:T(8,128)(2,1)S(1)}, u32[]{:S(2)}, u32[]{:S(2)}) %collective-permute-start.1) | collective-permute-done | bytes 262176 | tf_op jit(solution)/shard_map/ppermute | solution.py:592
  15.8 0.0 copy-start.5
  15.8 0.0 copy-done.4
  15.8 0.7 copy-done.5
  16.5 21.3 %layer.1 = (bf16[1024,512]{1,0:T(8,128)(2,1)}, bf16[256,2560]{1,0:T(8,128)(2,1)}) custom-call(s32[1]{0:T(128)} %bitcast.place_ref, s32[1,4]{1,0:T(1,128)} %lengths_ref.1, s32[4,4]{1,0:T(4,128)} %tiles_ref.1, bf16[256,512]{1,0:T(8,128)(2,1)} %ev_own.1, bf16[256,512]{1,0:T(8,128)(2,1)} %og_own.1, bf16[256,512]{1,0:T(8,128)(2,1)} %copy-done.4, ...), custom_call_target="tpu_custom_call" | custom-call | flops 10000000000 | bytes 8388608 | tf_op jit(solution)/shard_map/layer/pallas_call | solution.py:598
  37.7 0.0 copy-start
  37.7 1.3 %copy-done = bf16[256,2560]{1,0:T(8,128)(2,1)S(1)} copy-done((bf16[256,2560]{1,0:T(8,128)(2,1)S(1)}, bf16[256,2560]{1,0:T(8,128)(2,1)}, u32[]{:S(2)}) %copy-start) | copy-done | bytes 1310744
  39.1 0.0 copy-start.1
  39.1 1.2 %copy-done.1 = bf16[1024,512]{1,0:T(8,128)(2,1)S(1)} copy-done((bf16[1024,512]{1,0:T(8,128)(2,1)S(1)}, bf16[1024,512]{1,0:T(8,128)(2,1)}, u32[]{:S(2)}) %copy-start.1) | copy-done | bytes 1048600
  40.3 70.9 %exchange.1 = (bf16[1024,512]{1,0:T(8,128)(2,1)S(1)}, bf16[512,2560]{1,0:T(8,128)(2,1)S(1)}) custom-call(bf16[1024,512]{1,0:T(8,128)(2,1)S(1)} %copy-done.1, bf16[256,2560]{1,0:T(8,128)(2,1)S(1)} %copy-done), custom_call_target="tpu_custom_call" | custom-call | flops 1000000 | bytes 8388608 | tf_op jit(solution)/shard_map/exchange/pallas_call | solution.py:629
  111.2 0.0 copy-start.2
  111.2 1.0 copy-done.2
  112.2 0.1 fusion.14
  112.3 0.1 eq.39
  112.4 0.1 dynamic_update_slice.7
  112.5 0.1 eq.34
  112.6 1.1 slice_convert_fusion.1
  113.7 2.6 %slice_convert_fusion = f32[512,2048]{1,0:T(8,128)} fusion(bf16[512,2560]{1,0:T(8,128)(2,1)S(1)} %get-tuple-element.11), kind=kLoop, calls=%fused_computation | loop fusion | flops 1048576 | bytes 6291456 | tf_op jit(solution)/shard_map/convert_element_type | solution.py:669
  116.2 0.0 copy-start.3
  116.2 0.1 eq.41
  116.3 0.1 eq.36
  116.4 2.8 %fusion.3 = f32[384,512]{1,0:T(8,128)} fusion(bf16[1024,512]{1,0:T(8,128)(2,1)} %copy-done.2, s32[1024]{0:T(1024)S(1)} %eq.36, s32[384]{0:T(512)S(1)} %eq.34, pred[1024]{0:T(1024)(128)(4,1)S(1)} %broadcast_compare_fusion.1), kind=kOutput, calls=%fused_computation.4 | convolution fusion | flops 403439616 | bytes 1841664 | tf_op jit(solution)/shard_map/dot_general | solution.py:665
  119.2 0.0 copy-done.3
  119.2 1.5 %fusion = f32[384,512]{1,0:T(8,128)} fusion(bf16[1024,512]{1,0:T(8,128)(2,1)S(1)} %copy-done.3, s32[1024]{0:T(1024)S(1)} %eq.41, s32[384]{0:T(512)S(1)} %eq.39, pred[1024]{0:T(1024)(128)(4,1)S(1)} %broadcast_compare_fusion), kind=kOutput, calls=%fused_computation.1 | convolution fusion | flops 403439616 | bytes 1841664 | tf_op jit(solution)/shard_map/dot_general | solution.py:665
  (6 shorter events, 0.1 us)
Async XLA Ops:
  0.6 10.4 %collective-permute-start = (bf16[256,512]{1,0:T(8,128)(2,1)}, bf16[256,512]{1,0:T(8,128)(2,1)S(1)}, u32[]{:S(2)}, u32[]{:S(2)}) collective-permute-start(bf16[256,512]{1,0:T(8,128)(2,1)} %ev_own.1), channel_id=1, source_target_pairs={{0,1},{1,0},{2,3},{3,2},{4,5},{5,4},{6,7},{7,6},{8,9},{9,8},{10,11... | collective-permute-start | bytes 786440 | tf_op jit(solution)/shard_map/ppermute | solution.py:591
  3.6 12.1 %collective-permute-start.1 = (bf16[256,512]{1,0:T(8,128)(2,1)}, bf16[256,512]{1,0:T(8,128)(2,1)S(1)}, u32[]{:S(2)}, u32[]{:S(2)}) collective-permute-start(bf16[256,512]{1,0:T(8,128)(2,1)} %og_own.1), channel_id=1, source_target_pairs={{0,1},{1,0},{2,3},{3,2},{4,5},{5,4},{6,7},{7,6},{8,9},{9,8},{10,11... | collective-permute-start | bytes 786440 | tf_op jit(solution)/shard_map/ppermute | solution.py:592
  11.0 4.8 %copy-start.4 = (bf16[256,512]{1,0:T(8,128)(2,1)}, bf16[256,512]{1,0:T(8,128)(2,1)S(1)}, u32[]{:S(2)}) copy-start(bf16[256,512]{1,0:T(8,128)(2,1)S(1)} %collective-permute-done.ev_far) | copy-start | bytes 786436
  15.8 0.7 copy-start.5
  37.7 1.3 %copy-start = (bf16[256,2560]{1,0:T(8,128)(2,1)S(1)}, bf16[256,2560]{1,0:T(8,128)(2,1)}, u32[]{:S(2)}) copy-start(bf16[256,2560]{1,0:T(8,128)(2,1)} %get-tuple-element.9.refs_1_) | copy-start | bytes 3932164
  39.1 1.2 %copy-start.1 = (bf16[1024,512]{1,0:T(8,128)(2,1)S(1)}, bf16[1024,512]{1,0:T(8,128)(2,1)}, u32[]{:S(2)}) copy-start(bf16[1024,512]{1,0:T(8,128)(2,1)} %get-tuple-element.8.refs_0_) | copy-start | bytes 3145732
  111.2 1.0 copy-start.2
  116.2 3.0 %copy-start.3 = (bf16[1024,512]{1,0:T(8,128)(2,1)S(1)}, bf16[1024,512]{1,0:T(8,128)(2,1)}, u32[]{:S(2)}) copy-start(bf16[1024,512]{1,0:T(8,128)(2,1)} %copy-done.2) | copy-start | bytes 3145732

commit v2 on v1

--- a/solution.py
+++ b/solution.py
@@ -300,19 +300,61 @@
 
 
 def layer_kernel(
-    place_ref, lengths_ref, tiles_ref, ev_own, og_own, ev_far, og_far, weight_ref, out_weight_ref,
-    shards_ref, rows_ref, pack_ref, wgrad_ref,
-    ev, og, act, dact, att, slope, mixed, gm, mask, gp, gated,
+    data_size, lengths_ref, tiles_ref, ev_own, og_own, weight_ref, out_weight_ref,
+    shards_ref, rows_ref, got_ref, sum_ref,
+    ev, og, act, dact, att, slope, mixed, gm, mask, gp, gated, pack, chosen_slots, slot_numbers,
+    part_a, part_b, part_c, income_a, income_b, income_c, outgo_a, outgo_b, outgo_c,
+    totals_a, totals_b, totals_c,
+    local_sem, ctx_send, ctx_recv, row_send, row_recv, red_send, red_recv, all_send, all_recv,
 ):
     half, width = ev_own.shape
     full = 2 * half
-    place = place_ref[0]
+    data = lax.axis_index("dp")
+    place = lax.axis_index("ctx")
+    me = data * 2 + place
+    devices = data_size * 2
+    steps = data_size.bit_length() - 1
     own = pl.multiple_of(place * half, half)
     far = pl.multiple_of((1 - place) * half, half)
-    ev[pl.ds(own, half), :] = ev_own[...]
-    ev[pl.ds(far, half), :] = ev_far[...]
-    og[pl.ds(own, half), :] = og_own[...]
-    og[pl.ds(far, half), :] = og_far[...]
+    mine = pl.ds(own, half)
+    across_x = (data, 1 - place)
+    barrier = pltpu.get_barrier_semaphore()
+
+    def other(k):
+        to = lax.rem(me + k, devices)
+        return to, (to // 2, lax.rem(to, 2))
+
+    def remote(src, dst, send, recv, where):
+        return pltpu.make_async_remote_copy(
+            src_ref=src, dst_ref=dst, send_sem=send, recv_sem=recv, device_id=where,
+            device_id_type=MESH,
+        )
+
+    @pl.loop(1, devices)
+    def _(k):
+        _, where = other(k)
+        pl.semaphore_signal(barrier, inc=1, device_id=where, device_id_type=MESH)
+
+    pl.semaphore_wait(barrier, devices - 1)
+    ev_copy = remote(ev_own, ev.at[mine], ctx_send.at[0], ctx_recv.at[0], across_x)
+    og_copy = remote(og_own, og.at[mine], ctx_send.at[1], ctx_recv.at[1], across_x)
+    ev_copy.start()
+    og_copy.start()
+    ev[mine, :] = ev_own[...]
+    og[mine, :] = og_own[...]
+
+    def project(start):
+        rows = pl.ds(start, half)
+
+        @pl.loop(0, 4 * width // 256)
+        def _(n):
+            cols = pl.ds(pl.multiple_of(n * 256, 256), 256)
+            projected = jnp.dot(ev[rows, :], weight_ref[:, cols], preferred_element_type=F32)
+            sig = sigmoid_of(projected)
+            act[rows, cols] = (projected * sig).astype(BF16)
+            dact[rows, cols] = sig * (1.0 + projected * (1.0 - sig))
+
+    project(own)
 
     ends = []
     total = jnp.int32(0)
@@ -328,18 +370,37 @@
         for b in range(a + 1):
             col = b * TILE + lax.broadcasted_iota(jnp.int32, (TILE, TILE), 1)
             col_doc = sum((col >= e).astype(jnp.int32) for e in ends)
-            keep = jnp.where(tiles_ref[a, b] == 1, 1.0 / longest, 0.0)
+            keep = tiles_ref[a, b].astype(F32) / longest
             seen = (row_doc == col_doc) & (col <= row)
             mask[a * TILE : (a + 1) * TILE, b * TILE : (b + 1) * TILE] = jnp.where(seen, keep, 0.0)
 
-    @pl.loop(0, 4 * width // 256)
-    def _(n):
-        cols = pl.ds(pl.multiple_of(n * 256, 256), 256)
-        projected = jnp.dot(ev[...], weight_ref[:, cols], preferred_element_type=F32)
-        sig = sigmoid_of(projected)
-        value = projected * sig
-        act[:, cols] = value.astype(BF16)
-        dact[:, cols] = sig * (1.0 + projected * (1.0 - sig))
+    slots = pack.shape[0]
+    capacity = 3 * half // (2 * (slots // BLOCK))
+    early = lax.broadcasted_iota(jnp.int32, (half, half), 0) < lax.broadcasted_iota(
+        jnp.int32, (half, half), 1
+    )
+    slot = lax.broadcasted_iota(jnp.int32, (slots, half), 0)
+    spot = lax.broadcasted_iota(jnp.int32, (128, half), 0)
+    onehot = jnp.zeros((slots, half), F32)
+    numbers = jnp.zeros((slots, 128), F32)
+    for t in range(2):
+        shard = shards_ref[t : t + 1, :]
+        across = jnp.broadcast_to(shard.astype(F32), (half, half))
+        same = (jnp.transpose(across) == across) & early
+        rank = jnp.sum(same.astype(F32), axis=0, keepdims=True).astype(jnp.int32)
+        at = rank + t * capacity
+        onehot = onehot + (slot == shard * BLOCK + at).astype(F32)
+        number = rows_ref[t : t + 1, :]
+        high = (number // 256 + 1).astype(F32)
+        low = (number % 256).astype(F32)
+        left = jnp.where(slot == shard * BLOCK + 2 * capacity, high, 0.0) + jnp.where(
+            slot == shard * BLOCK + 2 * capacity + 1, low, 0.0
+        )
+        numbers = numbers + dot_rows(left.astype(BF16), (spot == at).astype(BF16))
+    chosen_slots[...] = onehot.astype(BF16)
+    slot_numbers[...] = numbers
+    ev_copy.wait_recv()
+    project(far)
 
     scale = 1.0 / math.sqrt(width // HEADS)
     head_width = width // HEADS
@@ -369,6 +430,8 @@
                 slope[p * 2 + h, lo:hi, :hi] = w * sig * (1.0 + scores * (1.0 - sig))
                 total = total + jnp.dot(a, only(v[:hi], h), preferred_element_type=F32)
             mixed[lo:hi, pl.ds(pl.multiple_of(p * 128, 128), 128)] = total
+
+    og_copy.wait_recv()
 
     @pl.loop(0, full // 128)
     def _(r):
@@ -391,8 +454,7 @@
             )
         ).astype(BF16)
 
-    @pl.loop(0, width // 128)
-    def _(p):
+    def back_pair(p):
         q = (act[:, pair_cols(2, p)].astype(F32) * scale).astype(BF16)
         k = act[:, pair_cols(3, p)]
         v = act[:, pair_cols(1, p)]
@@ -416,98 +478,123 @@
                 cols = pair_cols(base, p)
                 gp[lo:hi, cols] = (value * dact[lo:hi, cols]).astype(BF16)
 
-    mine = pl.ds(own, half)
-    wgrad_ref[:, 4 * width :] = dot_first(gated[:, mine], og[...]).astype(BF16)
-    ev_mine = ev[:, mine]
-
-    @pl.loop(0, 4 * width // 512)
-    def _(n):
-        cols = pl.ds(pl.multiple_of(n * 512, 512), 512)
-        wgrad_ref[:, cols] = dot_first(ev_mine, gp[:, cols]).astype(BF16)
-
-    grad_events = (og_own[...].astype(F32) + dot_rows(gp[mine, :], weight_ref[...])).astype(BF16)
-
-    slots = pack_ref.shape[0]
-    capacity = 3 * half // (2 * (slots // BLOCK))
-    early = lax.broadcasted_iota(jnp.int32, (half, half), 0) < lax.broadcasted_iota(
-        jnp.int32, (half, half), 1
-    )
-    slot = lax.broadcasted_iota(jnp.int32, (slots, half), 0)
-    spot = lax.broadcasted_iota(jnp.int32, (128, half), 0)
-    onehot = jnp.zeros((slots, half), F32)
-    numbers = jnp.zeros((slots, 128), F32)
-    for t in range(2):
-        shard = shards_ref[t : t + 1, :]
-        across = jnp.broadcast_to(shard.astype(F32), (half, half))
-        same = (jnp.transpose(across) == across) & early
-        rank = jnp.sum(same.astype(F32), axis=0, keepdims=True).astype(jnp.int32)
-        at = rank + t * capacity
-        onehot = onehot + (slot == shard * BLOCK + at).astype(F32)
-        number = rows_ref[t : t + 1, :]
-        high = (number // 256 + 1).astype(F32)
-        low = (number % 256).astype(F32)
-        left = jnp.where(slot == shard * BLOCK + 2 * capacity, high, 0.0) + jnp.where(
-            slot == shard * BLOCK + 2 * capacity + 1, low, 0.0
-        )
-        numbers = numbers + dot_rows(left.astype(BF16), (spot == at).astype(BF16))
-    onehot = onehot.astype(BF16)
-    packed = jnp.dot(onehot, grad_events, preferred_element_type=F32)
-    pack_ref[:, :128] = (packed[:, :128] + numbers).astype(BF16)
-    pack_ref[:, 128:] = packed[:, 128:].astype(BF16)
-
-
-def exchange_kernel(
-    data_size, pack_ref, wgrad_ref, got_ref, sum_ref,
-    totals, outgo, income, local_sem, row_send, row_recv, red_send, red_recv, all_send, all_recv,
-):
-    data = lax.axis_index("dp")
-    place = lax.axis_index("ctx")
-    me = data * 2 + place
-    devices = data_size * 2
-    barrier = pltpu.get_barrier_semaphore()
-
-    def other(k):
-        to = lax.rem(me + k, devices)
-        return to, (to // 2, lax.rem(to, 2))
-
-    @pl.loop(1, devices)
-    def _(k):
-        _, where = other(k)
-        pl.semaphore_signal(barrier, inc=1, device_id=where, device_id_type=MESH)
-
-    pl.semaphore_wait(barrier, devices - 1)
-
-    steps = data_size.bit_length() - 1
-    height = wgrad_ref.shape[0]
-
     def bit(n):
         return lax.rem(data // (1 << n), 2)
 
     def toward(n):
         return (data + (1 - 2 * bit(n)) * (1 << n), place)
 
-    def remote(src, dst, send, recv, where):
-        return pltpu.make_async_remote_copy(
-            src_ref=src, dst_ref=dst, send_sem=send, recv_sem=recv, device_id=where,
-            device_id_type=MESH,
-        )
-
-    def reduce_copy(n):
-        size = height >> (n + 1)
-        if n == 0:
-            src = wgrad_ref.at[pl.ds(pl.multiple_of((1 - bit(0)) * size, size), size)]
+    height = half
+
+    def travel(which, part, income, outgo, totals, left, last):
+        wide = part.shape[1]
+        columns = pl.ds(left, wide)
+
+        def halving(n):
+            size = height >> (n + 1)
+            if n == 0:
+                src = part.at[pl.ds(pl.multiple_of((1 - bit(0)) * size, size), size)]
+            else:
+                src = outgo.at[pl.ds(height - 2 * size, size)]
+            dst = income.at[pl.ds(height - 2 * size, size)]
+            return remote(src, dst, red_send.at[which, n], red_recv.at[which, n], toward(n))
+
+        sent = [halving(0)]
+        sent[0].start()
+        yield
+        offset = place * height
+        for n in range(steps):
+            size = height >> (n + 1)
+            came = pl.ds(height - 2 * size, size)
+            sent[n].wait_recv()
+            kept = pl.ds(pl.multiple_of(bit(n) * size, size), size)
+            held = part[kept, :].astype(F32) if n == 0 else totals[kept, :]
+            held = held + income[came, :].astype(F32)
+            offset = offset + bit(n) * size
+            if n + 1 < steps:
+                totals[:size, :] = held
+                small = size // 2
+                gone = pl.ds(pl.multiple_of((1 - bit(n + 1)) * small, small), small)
+                outgo[pl.ds(height - 2 * small, small), :] = totals[gone, :].astype(BF16)
+                sent.append(halving(n + 1))
+                sent[-1].start()
+                yield
+            else:
+                sum_ref[pl.ds(pl.multiple_of(offset, size), size), columns] = held.astype(BF16)
+
+        count = [0]
+
+        def spread(start, size, where):
+            rows = sum_ref.at[pl.ds(pl.multiple_of(start, 16), size), columns]
+            n = count[0]
+            count[0] += 1
+            copy = remote(rows, rows, all_send.at[which, n], all_recv.at[which, n], where)
+            copy.start()
+            sent.append(copy)
+            return copy
+
+        size = height >> steps
+        for n in range(steps - 1, 1, -1):
+            copy = spread(offset, size, toward(n))
+            yield
+            copy.wait_recv()
+            offset = offset - bit(n) * size
+            size = 2 * size
+        mirror = (1 - 2 * place) * height
+        if last == "x":
+            copy = spread(offset, size, toward(1))
+            yield
+            copy.wait_recv()
+            offset = offset - bit(1) * size
+            size = 2 * size
+            first = spread(offset, size, across_x)
+            near = spread(offset, size, toward(0))
+            yield
+            first.wait_recv()
+            back = spread(offset + mirror, size, toward(0))
+            yield
+            near.wait_recv()
+            back.wait_recv()
         else:
-            src = outgo.at[pl.ds(height - 2 * size, size)]
-        dst = income.at[pl.ds(height - 2 * size, size)]
-        return remote(src, dst, red_send.at[n], red_recv.at[n], toward(n))
-
-    first = reduce_copy(0)
-    first.start()
+            first = spread(offset, size, across_x)
+            second = spread(offset, size, toward(1))
+            yield
+            first.wait_recv()
+            third = spread(offset + mirror, size, toward(1))
+            yield
+            second.wait_recv()
+            offset = offset - bit(1) * size
+            size = 2 * size
+            near = spread(offset, size, toward(0))
+            third.wait_recv()
+            back = spread(offset + mirror, size, toward(0))
+            yield
+            near.wait_recv()
+            back.wait_recv()
+        for copy in sent:
+            copy.wait_send()
+
+    part_a[:, :width] = dot_first(gated[:, mine], og[...]).astype(BF16)
+    ev_mine = ev[:, mine]
+    part_a[:, width:] = dot_first(ev_mine, gp[:, :width]).astype(BF16)
+    run_a = travel(0, part_a, income_a, outgo_a, totals_a, 0, "x")
+    next(run_a)
+
+    pairs = width // 128
+    pl.loop(0, pairs // 2)(back_pair)
+    next(run_a)
+    pl.loop(pairs // 2, pairs)(back_pair)
+    next(run_a)
+
+    grad_events = (og_own[...].astype(F32) + dot_rows(gp[mine, :], weight_ref[...])).astype(BF16)
+    packed = jnp.dot(chosen_slots[...], grad_events, preferred_element_type=F32)
+    pack[:, :128] = (packed[:, :128] + slot_numbers[...]).astype(BF16)
+    pack[:, 128:] = packed[:, 128:].astype(BF16)
 
     def row_copy(k):
         to, where = other(k)
         return remote(
-            pack_ref.at[pl.ds(pl.multiple_of(to * BLOCK, BLOCK), BLOCK)],
+            pack.at[pl.ds(pl.multiple_of(to * BLOCK, BLOCK), BLOCK)],
             got_ref.at[pl.ds(pl.multiple_of(me * BLOCK, BLOCK), BLOCK)],
             row_send.at[k],
             row_recv.at[k],
@@ -515,60 +602,27 @@
         )
 
     here = pl.ds(pl.multiple_of(me * BLOCK, BLOCK), BLOCK)
-    local = pltpu.make_async_copy(pack_ref.at[here], got_ref.at[here], local_sem)
+    local = pltpu.make_async_copy(pack.at[here], got_ref.at[here], local_sem)
     local.start()
 
     @pl.loop(1, devices)
     def _(k):
         row_copy(k).start()
 
-    offset = place * height
-    for n in range(steps):
-        size = height >> (n + 1)
-        came = pl.ds(height - 2 * size, size)
-        reduce_copy(n).wait_recv()
-        kept = pl.ds(pl.multiple_of(bit(n) * size, size), size)
-        if n == 0:
-            held = wgrad_ref[kept, :].astype(F32)
-        else:
-            held = totals[kept, :]
-        held = held + income[came, :].astype(F32)
-        offset = offset + bit(n) * size
-        if n + 1 < steps:
-            totals[:size, :] = held
-            part = size // 2
-            gone = pl.ds(pl.multiple_of((1 - bit(n + 1)) * part, part), part)
-            outgo[pl.ds(height - 2 * part, part), :] = totals[gone, :].astype(BF16)
-            reduce_copy(n + 1).start()
-        else:
-            sum_ref[pl.ds(pl.multiple_of(offset, size), size), :] = held.astype(BF16)
-
-    def spread(n, start, size, where):
-        rows = sum_ref.at[pl.ds(pl.multiple_of(start, size), size)]
-        return remote(rows, rows, all_send.at[n], all_recv.at[n], where)
-
-    size = height >> steps
-    sent = []
-    for n in range(steps - 1, 0, -1):
-        copy = spread(n, offset, size, toward(n))
-        copy.start()
-        sent.append(copy)
-        copy.wait_recv()
-        offset = offset - bit(n) * size
-        size = 2 * size
-    ctx_copy = spread(steps, offset, size, (data, 1 - place))
-    ctx_copy.start()
-    near = spread(0, offset, size, toward(0))
-    near.start()
-    ctx_copy.wait_recv()
-    back = spread(steps + 1, offset + (1 - 2 * place) * height, size, toward(0))
-    back.start()
-    near.wait_recv()
-    back.wait_recv()
-    for copy in sent + [ctx_copy, near, back]:
-        copy.wait_send()
-    for n in range(steps):
-        reduce_copy(n).wait_send()
+    next(run_a)
+    third = part_b.shape[1]
+    part_b[...] = dot_first(ev_mine, gp[:, width : width + third]).astype(BF16)
+    run_b = travel(1, part_b, income_b, outgo_b, totals_b, 2 * width, "y")
+    next(run_b)
+    part_c[...] = dot_first(ev_mine, gp[:, width + third :]).astype(BF16)
+    run_c = travel(2, part_c, income_c, outgo_c, totals_c, 2 * width + third, "y")
+    next(run_c)
+    running = [run_a, run_b, run_c]
+    while running:
+        running = [run for run in running if next(run, "end") != "end"]
+
+    ev_copy.wait_send()
+    og_copy.wait_send()
     local.wait()
 
     @pl.loop(1, devices)
@@ -587,22 +641,20 @@
     devices = 2 * data_size
     capacity = 3 * half // (2 * devices)
     full = 2 * half
-    swap = [(0, 1), (1, 0)]
-    ev_far = lax.ppermute(events, "ctx", swap)
-    og_far = lax.ppermute(out_grad, "ctx", swap)
-    place = lax.axis_index("ctx").astype(jnp.int32).reshape(1)
     shards = jnp.stack([quotient_shard, remainder_shard])
     numbers = jnp.stack([quotient_row, remainder_row])
     vmem = pl.BlockSpec(memory_space=pltpu.VMEM)
     smem = pl.BlockSpec(memory_space=pltpu.SMEM)
-    packed, wgrad = pl.pallas_call(
-        layer_kernel,
+    steps = data_size.bit_length() - 1
+    wides = (2 * width, 3 * width // 2, 3 * width // 2)
+    got, sums = pl.pallas_call(
+        lambda *refs: layer_kernel(data_size, *refs),
         name="layer",
         out_shape=(
             jax.ShapeDtypeStruct((devices * BLOCK, width), BF16),
-            jax.ShapeDtypeStruct((half, 5 * width), BF16),
+            jax.ShapeDtypeStruct((full, 5 * width), BF16),
         ),
-        in_specs=[smem] * 3 + [vmem] * 8,
+        in_specs=[smem] * 2 + [vmem] * 6,
         out_specs=(vmem, vmem),
         scratch_shapes=[
             pltpu.VMEM((full, width), BF16),
@@ -616,42 +668,32 @@
             pltpu.VMEM((full, full), F32),
             pltpu.VMEM((full, 4 * width), BF16),
             pltpu.VMEM((full, width), BF16),
+            pltpu.VMEM((devices * BLOCK, width), BF16),
+            pltpu.VMEM((devices * BLOCK, half), BF16),
+            pltpu.VMEM((devices * BLOCK, 128), F32),
+            *[pltpu.VMEM((half, wide), BF16) for wide in wides],
+            *[pltpu.VMEM((half, wide), BF16) for wide in wides],
+            *[pltpu.VMEM((half, wide), BF16) for wide in wides],
+            *[pltpu.VMEM((half // 2, wide), F32) for wide in wides],
+            pltpu.SemaphoreType.DMA,
+            pltpu.SemaphoreType.DMA((2,)),
+            pltpu.SemaphoreType.DMA((2,)),
+            pltpu.SemaphoreType.DMA((devices,)),
+            pltpu.SemaphoreType.DMA((devices,)),
+            pltpu.SemaphoreType.DMA((3, steps)),
+            pltpu.SemaphoreType.DMA((3, steps)),
+            pltpu.SemaphoreType.DMA((3, steps + 3)),
+            pltpu.SemaphoreType.DMA((3, steps + 3)),
         ],
-        compiler_params=pltpu.CompilerParams(vmem_limit_bytes=56 * 2**20),
+        compiler_params=pltpu.CompilerParams(
+            collective_id=0, has_side_effects=True, vmem_limit_bytes=56 * 2**20
+        ),
         cost_estimate=pl.CostEstimate(
             flops=10 * 10**9, bytes_accessed=8 * 2**20, transcendentals=4 * 10**6
         ),
     )(
-        place, lengths, tile_mask, events, out_grad, ev_far, og_far, proj_weight, out_weight,
-        shards, numbers,
-    )
-    steps = data_size.bit_length() - 1
-    got, sums = pl.pallas_call(
-        lambda *refs: exchange_kernel(data_size, *refs),
-        name="exchange",
-        out_shape=(
-            jax.ShapeDtypeStruct((devices * BLOCK, width), BF16),
-            jax.ShapeDtypeStruct((full, 5 * width), BF16),
-        ),
-        in_specs=[vmem, vmem],
-        out_specs=(vmem, vmem),
-        scratch_shapes=[
-            pltpu.VMEM((half // 2, 5 * width), F32),
-            pltpu.VMEM((half, 5 * width), BF16),
-            pltpu.VMEM((half, 5 * width), BF16),
-            pltpu.SemaphoreType.DMA,
-            pltpu.SemaphoreType.DMA((devices,)),
-            pltpu.SemaphoreType.DMA((devices,)),
-            pltpu.SemaphoreType.DMA((steps,)),
-            pltpu.SemaphoreType.DMA((steps,)),
-            pltpu.SemaphoreType.DMA((steps + 2,)),
-            pltpu.SemaphoreType.DMA((steps + 2,)),
-        ],
-        compiler_params=pltpu.CompilerParams(
-            collective_id=0, has_side_effects=True, vmem_limit_bytes=40 * 2**20
-        ),
-        cost_estimate=pl.CostEstimate(flops=10**6, bytes_accessed=8 * 2**20, transcendentals=0),
-    )(packed, wgrad)
+        lengths, tile_mask, events, out_grad, proj_weight, out_weight, shards, numbers,
+    )
     blocks = got.reshape(devices, BLOCK, width)
     head = blocks[:, 2 * capacity : 2 * capacity + 2, : 2 * capacity].astype(jnp.int32)
     marks = jnp.where(head[:, 0] > 0, (head[:, 0] - 1) * 256 + head[:, 1], -1)
@@ -666,8 +708,8 @@
     return (
         grads[0],
         grads[1],
-        sums[:, : 4 * width].astype(F32),
-        sums[:, 4 * width :].astype(F32),
+        sums[:, width:].astype(F32),
+        sums[:, :width].astype(F32),
     )
 
 

time: 121 us -> 103 us (0.85)
  waiting for transfers between devices: 10.7 us -> 0 us
  local copies, waits for them, and re-layouts: 4.74 us -> 1.46 us
  starting transfers between devices: 3.08 us -> 0 us
    ppermute x2 -> x0, waiting for transfers between devices: 10.7 us -> none  [the longest x1 5.95 us: pair_body(): ev_far = lax.ppermute(events, 'ctx', swap)]
    unnamed x12 -> x4, local copies, waits for them, and re-layouts: 4.21 us -> 0.01 us
    ppermute x2 -> x0, starting transfers between devices: 3.08 us -> none  [the longest x1 3 us: pair_body(): ev_far = lax.ppermute(events, 'ctx', swap)]
    pallas_call x2 -> x1, Pallas kernels: 92.1 us -> 91.3 us  [pair_body(): pl.pallas_call(lambda *refs: layer_kernel(data_size, *refs), name='layer'...]
  transfers between devices with their start and end apart: 2 -> 0, of which waited for: 2 -> 0; matrix products, arithmetic and copies ran while one was open for 1% -> 0% of each run, Pallas kernels for 0% -> 0%
where the time goes in v2:
time: 103 us
  Pallas kernels  91.3 us (89%)
  other arithmetic  5.01 us (5%)
  matrix products  4.37 us (4%)
  local copies, waits for them, and re-layouts  1.46 us (1%)
    pallas_call x1, Pallas kernels, pair_body(): pl.pallas_call(lambda *refs: layer_kernel(data_size, *refs), name='layer'...  91.3 us
    dot_general x2, matrix products, pair_body(): grads.append(jnp.dot(matches.astype(BF16), got, preferred_element_type=F32))  4.37 us
    convert_element_type x1, other arithmetic, pair_body(): sums[:, width:].astype(F32)  2.56 us

profile of v2, /device:TPU:0, one launch (start us, length us, event | category | flops | bytes accessed | tf_op | source)
XLA Modules:
  0.0 102.8 jit_solution(9982124132207409423)
XLA Ops:
  0.6 1.3 %pad_add_fusion = (s32[2,256]{1,0:T(2,128)}, s32[2,256]{1,0:T(2,128)}) fusion(s32[1,256]{1,0:T(1,128)} %bitcast.9, s32[1,256]{1,0:T(1,128)} %bitcast.10, s32[1,256]{1,0:T(1,128)} %bitcast.11, s32[1,256]{1,0:T(1,128)} %bitcast.12), kind=kLoop, calls=%fused_computation.18 | loop fusion | flops 1024 | bytes 8192 | tf_op jit(solution)/shard_map/stack | solution.py:644
  1.9 91.3 %layer.1 = (bf16[1024,512]{1,0:T(8,128)(2,1)}, bf16[512,2560]{1,0:T(8,128)(2,1)}) custom-call(s32[1,4]{1,0:T(1,128)} %refs_0_.1, s32[4,4]{1,0:T(4,128)} %refs_1_.1, bf16[256,512]{1,0:T(8,128)(2,1)} %refs_2_.1, bf16[256,512]{1,0:T(8,128)(2,1)} %refs_3_.1, bf16[512,2048]{1,0:T(8,128)(2,1)} %refs_4_.1, bf16[512,512]{1,0:T(8,128)(2,1)} %refs_5_.1, ...), custom_call_target="tpu_custom_call" | custom-call | flops 10000000000 | bytes 8388608 | tf_op jit(solution)/shard_map/layer/pallas_call | solution.py:650
  93.2 0.0 copy-start.1
  93.2 0.9 slice.29
  94.2 0.1 fusion.14
  94.3 0.1 eq.39
  94.4 0.1 dynamic_update_slice.7
  94.5 0.1 eq.41
  94.5 0.1 eq.34
  94.7 0.1 eq.36
  94.7 0.0 copy-start
  94.7 2.9 %fusion.3 = f32[384,512]{1,0:T(8,128)} fusion(bf16[1024,512]{1,0:T(8,128)(2,1)} %get-tuple-element.6, s32[1024]{0:T(1024)S(1)} %eq.36, s32[384]{0:T(512)S(1)} %eq.34, pred[1024]{0:T(1024)(128)(4,1)S(1)} %broadcast_compare_fusion.1), kind=kOutput, calls=%fused_computation.4 | convolution fusion | flops 403439616 | bytes 1841664 | tf_op jit(solution)/shard_map/dot_general | solution.py:707
  97.6 0.0 copy-done.1
  97.6 1.5 %fusion = f32[384,512]{1,0:T(8,128)} fusion(bf16[1024,512]{1,0:T(8,128)(2,1)S(1)} %copy-done.1, s32[1024]{0:T(1024)S(1)} %eq.41, s32[384]{0:T(512)S(1)} %eq.39, pred[1024]{0:T(1024)(128)(4,1)S(1)} %broadcast_compare_fusion), kind=kOutput, calls=%fused_computation.1 | convolution fusion | flops 403439616 | bytes 1841664 | tf_op jit(solution)/shard_map/dot_general | solution.py:707
  99.1 0.0 copy-done
  99.1 1.1 %slice_convert_fusion.1 = f32[512,512]{1,0:T(8,128)} fusion(bf16[512,2560]{1,0:T(8,128)(2,1)S(1)} %copy-done), kind=kLoop, calls=%fused_computation.13 | loop fusion | flops 262144 | bytes 1572864 | tf_op jit(solution)/shard_map/convert_element_type | solution.py:712
  100.2 2.6 %slice_convert_fusion = f32[512,2048]{1,0:T(8,128)} fusion(bf16[512,2560]{1,0:T(8,128)(2,1)S(1)} %copy-done), kind=kLoop, calls=%fused_computation | loop fusion | flops 1048576 | bytes 6291456 | tf_op jit(solution)/shard_map/convert_element_type | solution.py:711
  (5 shorter events, 0.0 us)
Async XLA Ops:
  93.2 4.4 %copy-start.1 = (bf16[1024,512]{1,0:T(8,128)(2,1)S(1)}, bf16[1024,512]{1,0:T(8,128)(2,1)}, u32[]{:S(2)}) copy-start(bf16[1024,512]{1,0:T(8,128)(2,1)} %get-tuple-element.6) | copy-start | bytes 3145732
  94.7 4.4 %copy-start = (bf16[512,2560]{1,0:T(8,128)(2,1)S(1)}, bf16[512,2560]{1,0:T(8,128)(2,1)}, u32[]{:S(2)}) copy-start(bf16[512,2560]{1,0:T(8,128)(2,1)} %get-tuple-element.7) | copy-start | bytes 7864324

commit v3 on v2

--- a/solution.py
+++ b/solution.py
@@ -586,6 +586,16 @@
     pl.loop(pairs // 2, pairs)(back_pair)
     next(run_a)
 
+    third = part_b.shape[1]
+    part_b[...] = dot_first(ev_mine, gp[:, width : width + third]).astype(BF16)
+    run_b = travel(1, part_b, income_b, outgo_b, totals_b, 2 * width, "y")
+    next(run_b)
+    next(run_a)
+    part_c[...] = dot_first(ev_mine, gp[:, width + third :]).astype(BF16)
+    run_c = travel(2, part_c, income_c, outgo_c, totals_c, 2 * width + third, "y")
+    next(run_c)
+    next(run_a)
+
     grad_events = (og_own[...].astype(F32) + dot_rows(gp[mine, :], weight_ref[...])).astype(BF16)
     packed = jnp.dot(chosen_slots[...], grad_events, preferred_element_type=F32)
     pack[:, :128] = (packed[:, :128] + slot_numbers[...]).astype(BF16)
@@ -605,20 +615,12 @@
     local = pltpu.make_async_copy(pack.at[here], got_ref.at[here], local_sem)
     local.start()
 
-    @pl.loop(1, devices)
-    def _(k):
-        row_copy(k).start()
-
-    next(run_a)
-    third = part_b.shape[1]
-    part_b[...] = dot_first(ev_mine, gp[:, width : width + third]).astype(BF16)
-    run_b = travel(1, part_b, income_b, outgo_b, totals_b, 2 * width, "y")
-    next(run_b)
-    part_c[...] = dot_first(ev_mine, gp[:, width + third :]).astype(BF16)
-    run_c = travel(2, part_c, income_c, outgo_c, totals_c, 2 * width + third, "y")
-    next(run_c)
+    fourth = devices // 4
+    turns = [[k for k in (g + fourth, g + 2 * fourth, g + 3 * fourth, g) if k] for g in range(fourth)]
     running = [run_a, run_b, run_c]
-    while running:
+    while running or turns:
+        for k in turns.pop(0) if turns else []:
+            row_copy(k).start()
         running = [run for run in running if next(run, "end") != "end"]
 
     ev_copy.wait_send()

time: 103 us -> 93.5 us (0.908)
  Pallas kernels: 91.3 us -> 81.8 us
    pallas_call x1, Pallas kernels: 91.3 us -> 81.8 us  [pair_body(): pl.pallas_call(lambda *refs: layer_kernel(data_size, *refs), name='layer'...]
where the time goes in v3:
time: 93.5 us; the launch traced here: 93.3 us
  Pallas kernels  81.8 us (87%)
  other arithmetic  5.01 us (5%)
  matrix products  4.37 us (5%)
  local copies, waits for them, and re-layouts  1.46 us (2%)
    pallas_call x1, Pallas kernels, pair_body(): pl.pallas_call(lambda *refs: layer_kernel(data_size, *refs), name='layer'...  81.8 us
    dot_general x2, matrix products, pair_body(): grads.append(jnp.dot(matches.astype(BF16), got, preferred_element_type=F32))  4.37 us
    convert_element_type x1, other arithmetic, pair_body(): sums[:, width:].astype(F32)  2.56 us

profile of v3, /device:TPU:0, one launch (start us, length us, event | category | flops | bytes accessed | tf_op | source)
XLA Modules:
  0.0 93.3 jit_solution(13282597554443457821)
XLA Ops:
  0.6 1.3 %pad_add_fusion = (s32[2,256]{1,0:T(2,128)}, s32[2,256]{1,0:T(2,128)}) fusion(s32[1,256]{1,0:T(1,128)} %bitcast.9, s32[1,256]{1,0:T(1,128)} %bitcast.10, s32[1,256]{1,0:T(1,128)} %bitcast.11, s32[1,256]{1,0:T(1,128)} %bitcast.12), kind=kLoop, calls=%fused_computation.18 | loop fusion | flops 1024 | bytes 8192 | tf_op jit(solution)/shard_map/stack | solution.py:646
  1.9 81.8 %layer.1 = (bf16[1024,512]{1,0:T(8,128)(2,1)}, bf16[512,2560]{1,0:T(8,128)(2,1)}) custom-call(s32[1,4]{1,0:T(1,128)} %refs_0_.1, s32[4,4]{1,0:T(4,128)} %refs_1_.1, bf16[256,512]{1,0:T(8,128)(2,1)} %refs_2_.1, bf16[256,512]{1,0:T(8,128)(2,1)} %refs_3_.1, bf16[512,2048]{1,0:T(8,128)(2,1)} %refs_4_.1, bf16[512,512]{1,0:T(8,128)(2,1)} %refs_5_.1, ...), custom_call_target="tpu_custom_call" | custom-call | flops 10000000000 | bytes 8388608 | tf_op jit(solution)/shard_map/layer/pallas_call | solution.py:652
  83.7 0.0 copy-start.1
  83.7 0.9 %slice.29 = bf16[32,2,24]{2,1,0:T(2,128)(2,1)S(1)} slice(bf16[32,32,512]{2,1,0:T(8,128)(2,1)} %bitcast.13), slice={[0:32], [24:26], [0:24]} | slice | bytes 6144 | tf_op jit(solution)/shard_map/slice | solution.py:700
  84.7 0.1 fusion.14
  84.8 0.1 eq.39
  84.9 0.1 dynamic_update_slice.7
  84.9 0.1 eq.41
  85.0 0.1 eq.34
  85.2 0.1 eq.36
  85.2 0.0 copy-start
  85.2 2.9 %fusion.3 = f32[384,512]{1,0:T(8,128)} fusion(bf16[1024,512]{1,0:T(8,128)(2,1)} %get-tuple-element.6, s32[1024]{0:T(1024)S(1)} %eq.36, s32[384]{0:T(512)S(1)} %eq.34, pred[1024]{0:T(1024)(128)(4,1)S(1)} %broadcast_compare_fusion.1), kind=kOutput, calls=%fused_computation.4 | convolution fusion | flops 403439616 | bytes 1841664 | tf_op jit(solution)/shard_map/dot_general | solution.py:709
  88.1 0.0 copy-done.1
  88.1 1.5 %fusion = f32[384,512]{1,0:T(8,128)} fusion(bf16[1024,512]{1,0:T(8,128)(2,1)S(1)} %copy-done.1, s32[1024]{0:T(1024)S(1)} %eq.41, s32[384]{0:T(512)S(1)} %eq.39, pred[1024]{0:T(1024)(128)(4,1)S(1)} %broadcast_compare_fusion), kind=kOutput, calls=%fused_computation.1 | convolution fusion | flops 403439616 | bytes 1841664 | tf_op jit(solution)/shard_map/dot_general | solution.py:709
  89.6 0.0 copy-done
  89.6 1.1 %slice_convert_fusion.1 = f32[512,512]{1,0:T(8,128)} fusion(bf16[512,2560]{1,0:T(8,128)(2,1)S(1)} %copy-done), kind=kLoop, calls=%fused_computation.13 | loop fusion | flops 262144 | bytes 1572864 | tf_op jit(solution)/shard_map/convert_element_type | solution.py:714
  90.7 2.6 %slice_convert_fusion = f32[512,2048]{1,0:T(8,128)} fusion(bf16[512,2560]{1,0:T(8,128)(2,1)S(1)} %copy-done), kind=kLoop, calls=%fused_computation | loop fusion | flops 1048576 | bytes 6291456 | tf_op jit(solution)/shard_map/convert_element_type | solution.py:713
  (5 shorter events, 0.0 us)
Async XLA Ops:
  83.7 4.4 %copy-start.1 = (bf16[1024,512]{1,0:T(8,128)(2,1)S(1)}, bf16[1024,512]{1,0:T(8,128)(2,1)}, u32[]{:S(2)}) copy-start(bf16[1024,512]{1,0:T(8,128)(2,1)} %get-tuple-element.6) | copy-start | bytes 3145732
  85.2 4.4 %copy-start = (bf16[512,2560]{1,0:T(8,128)(2,1)S(1)}, bf16[512,2560]{1,0:T(8,128)(2,1)}, u32[]{:S(2)}) copy-start(bf16[512,2560]{1,0:T(8,128)(2,1)} %get-tuple-element.7) | copy-start | bytes 7864324

commit v4 on v3

--- a/solution.py
+++ b/solution.py
@@ -301,8 +301,8 @@
 
 def layer_kernel(
     data_size, lengths_ref, tiles_ref, ev_own, og_own, weight_ref, out_weight_ref,
-    shards_ref, rows_ref, got_ref, sum_ref,
-    ev, og, act, dact, att, slope, mixed, gm, mask, gp, gated, pack, chosen_slots, slot_numbers,
+    shards_ref, rows_ref, quotient_ref, remainder_ref, sum_ref,
+    ev, og, act, dact, att, slope, mixed, gm, mask, gp, gated, pack, got_ref, chosen_slots, slot_numbers,
     part_a, part_b, part_c, income_a, income_b, income_c, outgo_a, outgo_b, outgo_c,
     totals_a, totals_b, totals_c,
     local_sem, ctx_send, ctx_recv, row_send, row_recv, red_send, red_recv, all_send, all_recv,
@@ -313,7 +313,6 @@
     place = lax.axis_index("ctx")
     me = data * 2 + place
     devices = data_size * 2
-    steps = data_size.bit_length() - 1
     own = pl.multiple_of(place * half, half)
     far = pl.multiple_of((1 - place) * half, half)
     mine = pl.ds(own, half)
@@ -485,6 +484,7 @@
         return (data + (1 - 2 * bit(n)) * (1 << n), place)
 
     height = half
+    layers = data_size // 4
 
     def travel(which, part, income, outgo, totals, left, last):
         wide = part.shape[1]
@@ -503,7 +503,7 @@
         sent[0].start()
         yield
         offset = place * height
-        for n in range(steps):
+        for n in range(2):
             size = height >> (n + 1)
             came = pl.ds(height - 2 * size, size)
             sent[n].wait_recv()
@@ -511,16 +511,36 @@
             held = part[kept, :].astype(F32) if n == 0 else totals[kept, :]
             held = held + income[came, :].astype(F32)
             offset = offset + bit(n) * size
-            if n + 1 < steps:
-                totals[:size, :] = held
+            totals[:size, :] = held
+            if n == 0:
                 small = size // 2
-                gone = pl.ds(pl.multiple_of((1 - bit(n + 1)) * small, small), small)
+                gone = pl.ds(pl.multiple_of((1 - bit(1)) * small, small), small)
                 outgo[pl.ds(height - 2 * small, small), :] = totals[gone, :].astype(BF16)
-                sent.append(halving(n + 1))
-                sent[-1].start()
+                sent.append(halving(1))
+                sent[1].start()
                 yield
-            else:
-                sum_ref[pl.ds(pl.multiple_of(offset, size), size), columns] = held.astype(BF16)
+        size = height // data_size
+        low = height - height // 4
+        outgo[pl.ds(low, layers * size), :] = totals[: layers * size, :].astype(BF16)
+        layer = data // 4
+        for k in range(1, layers):
+            to = lax.rem(layer + k, layers)
+            src = outgo.at[pl.ds(pl.multiple_of(low + to * size, size), size)]
+            dst = income.at[pl.ds(low + (k - 1) * size, size)]
+            copy = remote(
+                src, dst, red_send.at[which, 1 + k], red_recv.at[which, 1 + k],
+                (to * 4 + lax.rem(data, 4), place),
+            )
+            copy.start()
+            sent.append(copy)
+        yield
+        held = totals[pl.ds(pl.multiple_of(layer * size, size), size), :]
+        for k in range(1, layers):
+            sent[1 + k].wait_recv()
+            held = held + income[pl.ds(low + (k - 1) * size, size), :].astype(F32)
+        region = offset
+        offset = offset + layer * size
+        sum_ref[pl.ds(pl.multiple_of(offset, size), size), columns] = held.astype(BF16)
 
         count = [0]
 
@@ -533,13 +553,15 @@
             sent.append(copy)
             return copy
 
-        size = height >> steps
-        for n in range(steps - 1, 1, -1):
-            copy = spread(offset, size, toward(n))
-            yield
+        copies = [
+            spread(offset, size, (lax.rem(layer + k, layers) * 4 + lax.rem(data, 4), place))
+            for k in range(1, layers)
+        ]
+        yield
+        for copy in copies:
             copy.wait_recv()
-            offset = offset - bit(n) * size
-            size = 2 * size
+        offset = region
+        size = layers * size
         mirror = (1 - 2 * place) * height
         if last == "x":
             copy = spread(offset, size, toward(1))
@@ -581,20 +603,26 @@
     next(run_a)
 
     pairs = width // 128
+    piece = width // 2
+
+    def late(part, which):
+        for n in range(3):
+            cols = slice((n + 1) * width + which * piece, (n + 1) * width + (which + 1) * piece)
+            part[:, n * piece : (n + 1) * piece] = dot_first(ev_mine, gp[:, cols]).astype(BF16)
+
     pl.loop(0, pairs // 2)(back_pair)
     next(run_a)
+    late(part_b, 0)
+    run_b = travel(1, part_b, income_b, outgo_b, totals_b, 2 * width, "y")
+    next(run_b)
     pl.loop(pairs // 2, pairs)(back_pair)
     next(run_a)
-
-    third = part_b.shape[1]
-    part_b[...] = dot_first(ev_mine, gp[:, width : width + third]).astype(BF16)
-    run_b = travel(1, part_b, income_b, outgo_b, totals_b, 2 * width, "y")
     next(run_b)
-    next(run_a)
-    part_c[...] = dot_first(ev_mine, gp[:, width + third :]).astype(BF16)
-    run_c = travel(2, part_c, income_c, outgo_c, totals_c, 2 * width + third, "y")
+    late(part_c, 1)
+    run_c = travel(2, part_c, income_c, outgo_c, totals_c, 2 * width + 3 * piece, "y")
     next(run_c)
     next(run_a)
+    next(run_b)
 
     grad_events = (og_own[...].astype(F32) + dot_rows(gp[mine, :], weight_ref[...])).astype(BF16)
     packed = jnp.dot(chosen_slots[...], grad_events, preferred_element_type=F32)
@@ -618,20 +646,55 @@
     fourth = devices // 4
     turns = [[k for k in (g + fourth, g + 2 * fourth, g + 3 * fourth, g) if k] for g in range(fourth)]
     running = [run_a, run_b, run_c]
-    while running or turns:
-        for k in turns.pop(0) if turns else []:
-            row_copy(k).start()
+    for count in (2, 2, 2, 1, 1, 0):
+        for _ in range(count):
+            for k in turns.pop(0):
+                row_copy(k).start()
+        running = [run for run in running if next(run, "end") != "end"]
+
+    local.wait()
+
+    @pl.loop(1, devices)
+    def _(k):
+        row_copy(k).wait_recv()
+
+    side = lax.broadcasted_iota(jnp.int32, (devices, slots), 0)
+    flat = lax.broadcasted_iota(jnp.int32, (devices, slots), 1)
+    found = []
+    for n in range(2):
+        pick = (flat == side * BLOCK + 2 * capacity + n).astype(BF16)
+        found.append(
+            jnp.dot(pick, got_ref[:, :128], preferred_element_type=F32).astype(BF16)
+        )
+
+    def keys_of(count, block, first):
+        row = lax.broadcasted_iota(jnp.int32, (count, devices), 0) // block
+        of = (row == lax.broadcasted_iota(jnp.int32, (count, devices), 1)).astype(BF16)
+        high = jnp.dot(of, found[0], preferred_element_type=F32)
+        low = jnp.dot(of, found[1], preferred_element_type=F32)
+        spot_row = lax.broadcasted_iota(jnp.int32, (count, 128), 0) % block + first
+        spot_lane = lax.broadcasted_iota(jnp.int32, (count, 128), 1)
+        key = jnp.where((spot_row == spot_lane) & (spot_lane < 2 * capacity), high * 256.0 + low, 0.0)
+        return jnp.sum(key, axis=1, keepdims=True)
+
+    column = jnp.broadcast_to(keys_of(slots, BLOCK, 0), (slots, 128))
+    line = jnp.transpose(column)[0:1, :]
+    spot_line = lax.broadcasted_iota(jnp.int32, (1, slots), 1) % BLOCK
+    for t, out in enumerate((quotient_ref, remainder_ref)):
+        wanted = keys_of(out.shape[0], capacity, t * capacity)
+        inside = (spot_line >= t * capacity) & (spot_line < (t + 1) * capacity) & (line > 0.0)
+        match = ((wanted == line) & inside).astype(BF16)
+        out[...] = jnp.dot(match, got_ref[...], preferred_element_type=F32)
+
+    while running:
         running = [run for run in running if next(run, "end") != "end"]
 
     ev_copy.wait_send()
     og_copy.wait_send()
-    local.wait()
 
     @pl.loop(1, devices)
     def _(k):
-        copy = row_copy(k)
-        copy.wait_send()
-        copy.wait_recv()
+        row_copy(k).wait_send()
 
 
 def pair_body(
@@ -647,17 +710,18 @@
     numbers = jnp.stack([quotient_row, remainder_row])
     vmem = pl.BlockSpec(memory_space=pltpu.VMEM)
     smem = pl.BlockSpec(memory_space=pltpu.SMEM)
-    steps = data_size.bit_length() - 1
+    layers = data_size // 4
     wides = (2 * width, 3 * width // 2, 3 * width // 2)
-    got, sums = pl.pallas_call(
+    quotient, remainder, sums = pl.pallas_call(
         lambda *refs: layer_kernel(data_size, *refs),
         name="layer",
         out_shape=(
-            jax.ShapeDtypeStruct((devices * BLOCK, width), BF16),
+            jax.ShapeDtypeStruct((devices * capacity, width), F32),
+            jax.ShapeDtypeStruct((devices * capacity, width), F32),
             jax.ShapeDtypeStruct((full, 5 * width), BF16),
         ),
         in_specs=[smem] * 2 + [vmem] * 6,
-        out_specs=(vmem, vmem),
+        out_specs=(vmem, vmem, vmem),
         scratch_shapes=[
             pltpu.VMEM((full, width), BF16),
             pltpu.VMEM((full, width), BF16),
@@ -671,6 +735,7 @@
             pltpu.VMEM((full, 4 * width), BF16),
             pltpu.VMEM((full, width), BF16),
             pltpu.VMEM((devices * BLOCK, width), BF16),
+            pltpu.VMEM((devices * BLOCK, width), BF16),
             pltpu.VMEM((devices * BLOCK, half), BF16),
             pltpu.VMEM((devices * BLOCK, 128), F32),
             *[pltpu.VMEM((half, wide), BF16) for wide in wides],
@@ -682,10 +747,10 @@
             pltpu.SemaphoreType.DMA((2,)),
             pltpu.SemaphoreType.DMA((devices,)),
             pltpu.SemaphoreType.DMA((devices,)),
-            pltpu.SemaphoreType.DMA((3, steps)),
-            pltpu.SemaphoreType.DMA((3, steps)),
-            pltpu.SemaphoreType.DMA((3, steps + 3)),
-            pltpu.SemaphoreType.DMA((3, steps + 3)),
+            pltpu.SemaphoreType.DMA((3, layers + 1)),
+            pltpu.SemaphoreType.DMA((3, layers + 1)),
+            pltpu.SemaphoreType.DMA((3, layers + 4)),
+            pltpu.SemaphoreType.DMA((3, layers + 4)),
         ],
         compiler_params=pltpu.CompilerParams(
             collective_id=0, has_side_effects=True, vmem_limit_bytes=56 * 2**20
@@ -696,21 +761,16 @@
     )(
         lengths, tile_mask, events, out_grad, proj_weight, out_weight, shards, numbers,
     )
-    blocks = got.reshape(devices, BLOCK, width)
-    head = blocks[:, 2 * capacity : 2 * capacity + 2, : 2 * capacity].astype(jnp.int32)
-    marks = jnp.where(head[:, 0] > 0, (head[:, 0] - 1) * 256 + head[:, 1], -1)
-    blank = jnp.full((devices, BLOCK), -1, jnp.int32)
-    grads = []
-    for t in range(2):
-        mine = marks[:, t * capacity : (t + 1) * capacity]
-        keys = lax.dynamic_update_slice(blank, mine, (0, t * capacity)).reshape(-1)
-        slots = mine.reshape(-1)
-        matches = (slots[:, None] == keys[None, :]) & (keys[None, :] >= 0)
-        grads.append(jnp.dot(matches.astype(BF16), got, preferred_element_type=F32))
+    piece = width // 2
+    proj_grad = [sums[:, 2 * piece : 4 * piece]]
+    for n in range(3):
+        for h in range(2):
+            start = (4 + 3 * h + n) * piece
+            proj_grad.append(sums[:, start : start + piece])
     return (
-        grads[0],
-        grads[1],
-        sums[:, width:].astype(F32),
+        quotient,
+        remainder,
+        jnp.concatenate(proj_grad, axis=1).astype(F32),
         sums[:, :width].astype(F32),
     )
 

time: 93.5 us -> 90.9 us (0.972)
  matrix products: 4.37 us -> 0 us
  local copies, waits for them, and re-layouts: 1.46 us -> 3.67 us
  Pallas kernels: 81.8 us -> 80.1 us
  other arithmetic: 5.01 us -> 6.16 us
    dot_general x2 -> x0, matrix products: 4.37 us -> none  [pair_body(): grads.append(jnp.dot(matches.astype(BF16), got, preferred_element_type=F32))]
    unnamed x4 -> x13, local copies, waits for them, and re-layouts: 0.01 us -> 3.63 us
    pallas_call x1, Pallas kernels: 81.8 us -> 80.1 us  [pair_body(): pl.pallas_call(lambda *refs: layer_kernel(data_size, *refs), name='layer'...]
    convert_element_type x1, other arithmetic: 1.1 us -> 2.3 us  [pair_body(): sums[:, :width].astype(F32)]
    slice x2 -> x0, local copies, waits for them, and re-layouts: 1.01 us -> none  [the longest x1 0.94 us: pair_body(): blocks[:, 2 * capacity:2 * capacity + 2, :2 * capacity].astype(jnp.int32)]
    convert_element_type x2 -> x1, other arithmetic: 2.57 us -> 2.54 us  [pair_body(): jnp.concatenate(proj_grad, axis=1).astype(F32)]
where the time goes in v4:
time: 90.9 us; the launch traced here: 90.6 us
  Pallas kernels  80.1 us (88%)
  other arithmetic  6.16 us (7%)
  local copies, waits for them, and re-layouts  3.67 us (4%)
    pallas_call x1, Pallas kernels, pair_body(): pl.pallas_call(lambda *refs: layer_kernel(data_size, *refs), name='layer'...  80.1 us
    unnamed x13, local copies, waits for them, and re-layouts  3.63 us
    convert_element_type x1, other arithmetic, pair_body(): jnp.concatenate(proj_grad, axis=1).astype(F32)  2.54 us
    convert_element_type x1, other arithmetic, pair_body(): sums[:, :width].astype(F32)  2.3 us

profile of v4, /device:TPU:0, one launch (start us, length us, event | category | flops | bytes accessed | tf_op | source)
XLA Modules:
  0.0 90.6 jit_solution(10981666073253969320)
XLA Ops:
  0.6 1.3 %pad_add_fusion = (s32[2,256]{1,0:T(2,128)}, s32[2,256]{1,0:T(2,128)}) fusion(s32[1,256]{1,0:T(1,128)} %bitcast.4, s32[1,256]{1,0:T(1,128)} %bitcast.5, s32[1,256]{1,0:T(1,128)} %bitcast.6, s32[1,256]{1,0:T(1,128)} %bitcast.7), kind=kLoop, calls=%fused_computation.7 | loop fusion | flops 1024 | bytes 8192 | tf_op jit(solution)/shard_map/stack | solution.py:709
  1.9 80.1 %layer.1 = (f32[384,512]{1,0:T(8,128)}, f32[384,512]{1,0:T(8,128)}, bf16[512,2560]{1,0:T(8,128)(2,1)}) custom-call(s32[1,4]{1,0:T(1,128)} %refs_0_.1, s32[4,4]{1,0:T(4,128)} %refs_1_.1, bf16[256,512]{1,0:T(8,128)(2,1)} %refs_2_.1, bf16[256,512]{1,0:T(8,128)(2,1)} %refs_3_.1, bf16[512,2048]{1,0:T(8,128)(2,1)} %refs_4_.1, bf16[512,512]{1,0:T(8,128)(2,1)} %refs_5_.1, ...), custom_call_target="tpu_custom_call" | custom-call | flops 10000000000 | bytes 8388608 | tf_op jit(solution)/shard_map/layer/pallas_call | solution.py:715
  82.0 0.0 copy-start
  82.0 2.3 %slice_convert_fusion = f32[512,512]{1,0:T(8,128)} fusion(bf16[512,2560]{1,0:T(8,128)(2,1)} %get-tuple-element.9), kind=kLoop, calls=%fused_computation.1 | loop fusion | flops 262144 | bytes 1572864 | tf_op jit(solution)/shard_map/convert_element_type | solution.py:774
  84.3 1.2 %slice_dynamic-update-slice_fusion = bf16[512,2048]{1,0:T(8,128)(2,1)S(1)} fusion(bf16[512,2560]{1,0:T(8,128)(2,1)} %get-tuple-element.9), kind=kLoop, calls=%fused_computation | loop fusion | bytes 1572864
  85.6 0.0 copy-done
  85.8 0.0 copy-start.2
  85.8 2.5 %convert_element_type.6 = f32[512,2048]{1,0:T(8,128)} convert(bf16[512,2048]{1,0:T(8,128)(2,1)S(1)} %slice_dynamic-update-slice_fusion.1) | non-fusion elementwise | flops 1048576 | bytes 6291456 | tf_op jit(solution)/shard_map/convert_element_type | solution.py:773
  88.3 0.0 copy-done.2
  88.3 0.0 copy-start.1
  88.3 0.9 copy.21
  89.2 0.5 copy-done.1
  89.7 0.9 copy.22
  (5 shorter events, 0.1 us)
Async XLA Ops:
  82.0 3.5 %copy-start = (bf16[512,2560]{1,0:T(8,128)(2,1)S(1)}, bf16[512,2560]{1,0:T(8,128)(2,1)}, u32[]{:S(2)}) copy-start(bf16[512,2560]{1,0:T(8,128)(2,1)} %get-tuple-element.9) | copy-start | bytes 7864324
  85.8 2.6 %copy-start.2 = (f32[384,512]{1,0:T(8,128)S(1)}, f32[384,512]{1,0:T(8,128)}, u32[]{:S(2)}) copy-start(f32[384,512]{1,0:T(8,128)} %get-tuple-element.16) | copy-start | bytes 2359300
  88.3 1.4 %copy-start.1 = (f32[384,512]{1,0:T(8,128)S(1)}, f32[384,512]{1,0:T(8,128)}, u32[]{:S(2)}) copy-start(f32[384,512]{1,0:T(8,128)} %get-tuple-element.17) | copy-start | bytes 2359300

commit v5 on v4

--- a/solution.py
+++ b/solution.py
@@ -283,8 +283,7 @@
 F32 = jnp.float32
 BF16 = jnp.bfloat16
 MESH = pl.DeviceIdType.MESH
-BLOCK = 32
-WIDTH = 512
+MARK = 16
 
 
 def dot_rows(a, b):
@@ -301,11 +300,11 @@
 
 def layer_kernel(
     data_size, lengths_ref, tiles_ref, ev_own, og_own, weight_ref, out_weight_ref,
-    shards_ref, rows_ref, quotient_ref, remainder_ref, sum_ref,
-    ev, og, act, dact, att, slope, mixed, gm, mask, gp, gated, pack, got_ref, chosen_slots, slot_numbers,
+    info_ref, quotient_ref, remainder_ref, sum_ref,
+    ev, og, act, dact, att, slope, mixed, gm, mask, gp, gated, pack, got_ref, info, chosen_slots, marks, marks_in,
     part_a, part_b, part_c, income_a, income_b, income_c, outgo_a, outgo_b, outgo_c,
     totals_a, totals_b, totals_c,
-    local_sem, ctx_send, ctx_recv, row_send, row_recv, red_send, red_recv, all_send, all_recv,
+    local_sem, ctx_send, ctx_recv, row_send, row_recv, mark_send, mark_recv, red_send, red_recv, all_send, all_recv,
 ):
     half, width = ev_own.shape
     full = 2 * half
@@ -320,8 +319,8 @@
     barrier = pltpu.get_barrier_semaphore()
 
     def other(k):
-        to = lax.rem(me + k, devices)
-        return to, (to // 2, lax.rem(to, 2))
+        to = lax.rem(data + k, data_size)
+        return to, (to, place)
 
     def remote(src, dst, send, recv, where):
         return pltpu.make_async_remote_copy(
@@ -329,12 +328,18 @@
             device_id_type=MESH,
         )
 
-    @pl.loop(1, devices)
+    pl.semaphore_signal(barrier, inc=1, device_id=across_x, device_id_type=MESH)
+
+    @pl.loop(1, data_size)
     def _(k):
         _, where = other(k)
         pl.semaphore_signal(barrier, inc=1, device_id=where, device_id_type=MESH)
 
-    pl.semaphore_wait(barrier, devices - 1)
+    pl.semaphore_wait(barrier, data_size)
+    my_info = pl.ds(pl.multiple_of(place * 8, 8), 8)
+    info_copy = remote(info_ref, info.at[my_info], ctx_send.at[2], ctx_recv.at[2], across_x)
+    info_copy.start()
+    info[my_info, :] = info_ref[...]
     ev_copy = remote(ev_own, ev.at[mine], ctx_send.at[0], ctx_recv.at[0], across_x)
     og_copy = remote(og_own, og.at[mine], ctx_send.at[1], ctx_recv.at[1], across_x)
     ev_copy.start()
@@ -373,31 +378,60 @@
             seen = (row_doc == col_doc) & (col <= row)
             mask[a * TILE : (a + 1) * TILE, b * TILE : (b + 1) * TILE] = jnp.where(seen, keep, 0.0)
 
+    info_copy.wait_recv()
     slots = pack.shape[0]
-    capacity = 3 * half // (2 * (slots // BLOCK))
+    capacity = 3 * half // (2 * devices)
+    block = 4 * capacity
     early = lax.broadcasted_iota(jnp.int32, (half, half), 0) < lax.broadcasted_iota(
         jnp.int32, (half, half), 1
     )
     slot = lax.broadcasted_iota(jnp.int32, (slots, half), 0)
+    mark_row = lax.broadcasted_iota(jnp.int32, (data_size * MARK, half), 0)
     spot = lax.broadcasted_iota(jnp.int32, (128, half), 0)
-    onehot = jnp.zeros((slots, half), F32)
-    numbers = jnp.zeros((slots, 128), F32)
-    for t in range(2):
-        shard = shards_ref[t : t + 1, :]
-        across = jnp.broadcast_to(shard.astype(F32), (half, half))
-        same = (jnp.transpose(across) == across) & early
-        rank = jnp.sum(same.astype(F32), axis=0, keepdims=True).astype(jnp.int32)
-        at = rank + t * capacity
-        onehot = onehot + (slot == shard * BLOCK + at).astype(F32)
-        number = rows_ref[t : t + 1, :]
-        high = (number // 256 + 1).astype(F32)
-        low = (number % 256).astype(F32)
-        left = jnp.where(slot == shard * BLOCK + 2 * capacity, high, 0.0) + jnp.where(
-            slot == shard * BLOCK + 2 * capacity + 1, low, 0.0
+    numbers = jnp.zeros((data_size * MARK, 128), F32)
+    for side in range(2):
+        onehot = jnp.zeros((slots, half), F32)
+        for t in range(2):
+            shard = info[side * 8 + t : side * 8 + t + 1, :]
+            across = jnp.broadcast_to(shard.astype(F32), (half, half))
+            same = (jnp.transpose(across) == across) & early
+            rank = jnp.sum(same.astype(F32), axis=0, keepdims=True).astype(jnp.int32)
+            at = rank + (2 * side + t) * capacity
+            owner = jnp.where(shard % 2 == place, shard // 2, -100)
+            onehot = onehot + (slot == owner * block + at).astype(F32)
+            number = info[side * 8 + 2 + t : side * 8 + 3 + t, :]
+            high = (number // 256 + 1).astype(F32)
+            low = (number % 256).astype(F32)
+            left = jnp.where(mark_row == owner * MARK, high, 0.0) + jnp.where(
+                mark_row == owner * MARK + 1, low, 0.0
+            )
+            numbers = numbers + dot_rows(left.astype(BF16), (spot == at).astype(BF16))
+        chosen_slots[:, side * half : (side + 1) * half] = onehot.astype(BF16)
+    marks[...] = numbers.astype(BF16)
+
+    def block_copy(k, src, dst, size, send, recv):
+        to, where = other(k)
+        return remote(
+            src.at[pl.ds(pl.multiple_of(to * size, size), size)],
+            dst.at[pl.ds(pl.multiple_of(data * size, size), size)],
+            send.at[k],
+            recv.at[k],
+            where,
         )
-        numbers = numbers + dot_rows(left.astype(BF16), (spot == at).astype(BF16))
-    chosen_slots[...] = onehot.astype(BF16)
-    slot_numbers[...] = numbers
+
+    def mark_copy(k):
+        return block_copy(k, marks, marks_in, MARK, mark_send, mark_recv)
+
+    def row_copy(k):
+        return block_copy(k, pack, got_ref, block, row_send, row_recv)
+
+    @pl.loop(1, data_size)
+    def _(k):
+        mark_copy(k).start()
+
+    marks_here = pl.ds(pl.multiple_of(data * MARK, MARK), MARK)
+    marks_in[marks_here, :] = marks[marks_here, :]
+
     ev_copy.wait_recv()
     project(far)
 
@@ -624,29 +658,16 @@
     next(run_a)
     next(run_b)
 
-    grad_events = (og_own[...].astype(F32) + dot_rows(gp[mine, :], weight_ref[...])).astype(BF16)
-    packed = jnp.dot(chosen_slots[...], grad_events, preferred_element_type=F32)
-    pack[:, :128] = (packed[:, :128] + slot_numbers[...]).astype(BF16)
-    pack[:, 128:] = packed[:, 128:].astype(BF16)
-
-    def row_copy(k):
-        to, where = other(k)
-        return remote(
-            pack.at[pl.ds(pl.multiple_of(to * BLOCK, BLOCK), BLOCK)],
-            got_ref.at[pl.ds(pl.multiple_of(me * BLOCK, BLOCK), BLOCK)],
-            row_send.at[k],
-            row_recv.at[k],
-            where,
-        )
-
-    here = pl.ds(pl.multiple_of(me * BLOCK, BLOCK), BLOCK)
+    grad_events = (og[...].astype(F32) + dot_rows(gp[...], weight_ref[...])).astype(BF16)
+    pack[...] = jnp.dot(chosen_slots[...], grad_events, preferred_element_type=F32).astype(BF16)
+    here = pl.ds(pl.multiple_of(data * block, block), block)
     local = pltpu.make_async_copy(pack.at[here], got_ref.at[here], local_sem)
     local.start()
 
-    fourth = devices // 4
+    fourth = data_size // 4
     turns = [[k for k in (g + fourth, g + 2 * fourth, g + 3 * fourth, g) if k] for g in range(fourth)]
     running = [run_a, run_b, run_c]
-    for count in (2, 2, 2, 1, 1, 0):
+    for count in (1, 1, 1, 1, 0, 0):
         for _ in range(count):
             for k in turns.pop(0):
                 row_copy(k).start()
@@ -654,34 +675,37 @@
 
     local.wait()
 
-    @pl.loop(1, devices)
+    @pl.loop(1, data_size)
     def _(k):
         row_copy(k).wait_recv()
-
-    side = lax.broadcasted_iota(jnp.int32, (devices, slots), 0)
-    flat = lax.broadcasted_iota(jnp.int32, (devices, slots), 1)
+        mark_copy(k).wait_recv()
+
+    sender = lax.broadcasted_iota(jnp.int32, (data_size, data_size * MARK), 0)
+    flat = lax.broadcasted_iota(jnp.int32, (data_size, data_size * MARK), 1)
     found = []
     for n in range(2):
-        pick = (flat == side * BLOCK + 2 * capacity + n).astype(BF16)
-        found.append(
-            jnp.dot(pick, got_ref[:, :128], preferred_element_type=F32).astype(BF16)
-        )
-
-    def keys_of(count, block, first):
-        row = lax.broadcasted_iota(jnp.int32, (count, devices), 0) // block
-        of = (row == lax.broadcasted_iota(jnp.int32, (count, devices), 1)).astype(BF16)
+        pick = (flat == sender * MARK + n).astype(BF16)
+        found.append(jnp.dot(pick, marks_in[...], preferred_element_type=F32).astype(BF16))
+
+    def keys_of(count, per, lane_of):
+        row = lax.broadcasted_iota(jnp.int32, (count, data_size), 0) // per
+        of = (row == lax.broadcasted_iota(jnp.int32, (count, data_size), 1)).astype(BF16)
         high = jnp.dot(of, found[0], preferred_element_type=F32)
         low = jnp.dot(of, found[1], preferred_element_type=F32)
-        spot_row = lax.broadcasted_iota(jnp.int32, (count, 128), 0) % block + first
+        spot_row = lane_of(lax.broadcasted_iota(jnp.int32, (count, 128), 0) % per)
         spot_lane = lax.broadcasted_iota(jnp.int32, (count, 128), 1)
-        key = jnp.where((spot_row == spot_lane) & (spot_lane < 2 * capacity), high * 256.0 + low, 0.0)
+        key = jnp.where(spot_row == spot_lane, high * 256.0 + low, 0.0)
         return jnp.sum(key, axis=1, keepdims=True)
 
-    column = jnp.broadcast_to(keys_of(slots, BLOCK, 0), (slots, 128))
+    column = jnp.broadcast_to(keys_of(slots, block, lambda at: at), (slots, 128))
     line = jnp.transpose(column)[0:1, :]
-    spot_line = lax.broadcasted_iota(jnp.int32, (1, slots), 1) % BLOCK
+    spot_line = lax.broadcasted_iota(jnp.int32, (1, slots), 1) % (2 * capacity)
     for t, out in enumerate((quotient_ref, remainder_ref)):
-        wanted = keys_of(out.shape[0], capacity, t * capacity)
+        wanted = keys_of(
+            out.shape[0],
+            2 * capacity,
+            lambda at: at + t * capacity + jnp.where(at >= capacity, capacity, 0),
+        )
         inside = (spot_line >= t * capacity) & (spot_line < (t + 1) * capacity) & (line > 0.0)
         match = ((wanted == line) & inside).astype(BF16)
         out[...] = jnp.dot(match, got_ref[...], preferred_element_type=F32)
@@ -692,9 +716,12 @@
     ev_copy.wait_send()
     og_copy.wait_send()
 
-    @pl.loop(1, devices)
+    info_copy.wait_send()
+
+    @pl.loop(1, data_size)
     def _(k):
         row_copy(k).wait_send()
+        mark_copy(k).wait_send()
 
 
 def pair_body(
@@ -706,8 +733,8 @@
     devices = 2 * data_size
     capacity = 3 * half // (2 * devices)
     full = 2 * half
-    shards = jnp.stack([quotient_shard, remainder_shard])
-    numbers = jnp.stack([quotient_row, remainder_row])
+    named = [quotient_shard, remainder_shard, quotient_row, remainder_row]
+    info = jnp.stack(named + named)
     vmem = pl.BlockSpec(memory_space=pltpu.VMEM)
     smem = pl.BlockSpec(memory_space=pltpu.SMEM)
     layers = data_size // 4
@@ -720,7 +747,7 @@
             jax.ShapeDtypeStruct((devices * capacity, width), F32),
             jax.ShapeDtypeStruct((full, 5 * width), BF16),
         ),
-        in_specs=[smem] * 2 + [vmem] * 6,
+        in_specs=[smem] * 2 + [vmem] * 5,
         out_specs=(vmem, vmem, vmem),
         scratch_shapes=[
             pltpu.VMEM((full, width), BF16),
@@ -734,19 +761,23 @@
             pltpu.VMEM((full, full), F32),
             pltpu.VMEM((full, 4 * width), BF16),
             pltpu.VMEM((full, width), BF16),
-            pltpu.VMEM((devices * BLOCK, width), BF16),
-            pltpu.VMEM((devices * BLOCK, width), BF16),
-            pltpu.VMEM((devices * BLOCK, half), BF16),
-            pltpu.VMEM((devices * BLOCK, 128), F32),
+            pltpu.VMEM((data_size * 4 * capacity, width), BF16),
+            pltpu.VMEM((data_size * 4 * capacity, width), BF16),
+            pltpu.VMEM((16, half), jnp.int32),
+            pltpu.VMEM((data_size * 4 * capacity, full), BF16),
+            pltpu.VMEM((data_size * MARK, 128), BF16),
+            pltpu.VMEM((data_size * MARK, 128), BF16),
             *[pltpu.VMEM((half, wide), BF16) for wide in wides],
             *[pltpu.VMEM((half, wide), BF16) for wide in wides],
             *[pltpu.VMEM((half, wide), BF16) for wide in wides],
             *[pltpu.VMEM((half // 2, wide), F32) for wide in wides],
             pltpu.SemaphoreType.DMA,
-            pltpu.SemaphoreType.DMA((2,)),
-            pltpu.SemaphoreType.DMA((2,)),
-            pltpu.SemaphoreType.DMA((devices,)),
-            pltpu.SemaphoreType.DMA((devices,)),
+            pltpu.SemaphoreType.DMA((3,)),
+            pltpu.SemaphoreType.DMA((3,)),
+            pltpu.SemaphoreType.DMA((data_size,)),
+            pltpu.SemaphoreType.DMA((data_size,)),
+            pltpu.SemaphoreType.DMA((data_size,)),
+            pltpu.SemaphoreType.DMA((data_size,)),
             pltpu.SemaphoreType.DMA((3, layers + 1)),
             pltpu.SemaphoreType.DMA((3, layers + 1)),
             pltpu.SemaphoreType.DMA((3, layers + 4)),
@@ -759,7 +790,7 @@
             flops=10 * 10**9, bytes_accessed=8 * 2**20, transcendentals=4 * 10**6
         ),
     )(
-        lengths, tile_mask, events, out_grad, proj_weight, out_weight, shards, numbers,
+        lengths, tile_mask, events, out_grad, proj_weight, out_weight, info,
     )
     piece = width // 2
     proj_grad = [sums[:, 2 * piece : 4 * piece]]

time: 90.9 us -> 85.5 us (0.941)
  Pallas kernels: 80.1 us -> 74.7 us
  local copies, waits for them, and re-layouts: 3.67 us -> 5.07 us
  other arithmetic: 6.16 us -> 4.84 us
    pallas_call x1, Pallas kernels: 80.1 us -> 74.7 us  [pair_body(): pl.pallas_call(lambda *refs: layer_kernel(data_size, *refs), name='layer'...]
    another operation x0 -> x1, local copies, waits for them, and re-layouts: none -> 1.41 us  [pair_body(): info = jnp.stack(named + named)]
    another operation x1 -> x0, other arithmetic: 1.32 us -> none  [pair_body(): shards = jnp.stack([quotient_shard, remainder_shard])]
where the time goes in v5:
time: 85.5 us; the launch traced here: 85.3 us
  Pallas kernels  74.7 us (87%)
  local copies, waits for them, and re-layouts  5.07 us (6%)
  other arithmetic  4.84 us (6%)
    pallas_call x1, Pallas kernels, pair_body(): pl.pallas_call(lambda *refs: layer_kernel(data_size, *refs), name='layer'...  74.7 us
    unnamed x13, local copies, waits for them, and re-layouts  3.63 us
    convert_element_type x1, other arithmetic, pair_body(): jnp.concatenate(proj_grad, axis=1).astype(F32)  2.54 us
    convert_element_type x1, other arithmetic, pair_body(): sums[:, :width].astype(F32)  2.3 us

profile of v5, /device:TPU:0, one launch (start us, length us, event | category | flops | bytes accessed | tf_op | source)
XLA Modules:
  0.0 85.3 jit_solution(14300028172618522964)
XLA Ops:
  0.6 1.4 %stack.23.refs_6_ = s32[8,256]{1,0:T(8,128)} concatenate(s32[1,256]{1,0:T(1,128)} %bitcast.4, s32[1,256]{1,0:T(1,128)} %bitcast.6, s32[1,256]{1,0:T(1,128)} %bitcast.8, s32[1,256]{1,0:T(1,128)} %bitcast.10, s32[1,256]{1,0:T(1,128)} %bitcast.5, s32[1,256]{1,0:T(1,128)} %bitcast.7, s32[1,256]{1,0:T(1,128)} %bitcast.9, s32[1,256]{1,0:T(1,128)} %bitcast.11), dimensions={0} | concatenate | bytes 16384 | tf_op jit(solution)/shard_map/stack | solution.py:737
  2.0 74.7 %layer.1 = (f32[384,512]{1,0:T(8,128)}, f32[384,512]{1,0:T(8,128)}, bf16[512,2560]{1,0:T(8,128)(2,1)}) custom-call(s32[1,4]{1,0:T(1,128)} %refs_0_.1, s32[4,4]{1,0:T(4,128)} %refs_1_.1, bf16[256,512]{1,0:T(8,128)(2,1)} %refs_2_.1, bf16[256,512]{1,0:T(8,128)(2,1)} %refs_3_.1, bf16[512,2048]{1,0:T(8,128)(2,1)} %refs_4_.1, bf16[512,512]{1,0:T(8,128)(2,1)} %refs_5_.1, ...), custom_call_target="tpu_custom_call" | custom-call | flops 10000000000 | bytes 8388608 | tf_op jit(solution)/shard_map/layer/pallas_call | solution.py:742
  76.7 0.0 copy-start
  76.7 2.3 %slice_convert_fusion = f32[512,512]{1,0:T(8,128)} fusion(bf16[512,2560]{1,0:T(8,128)(2,1)} %get-tuple-element.9), kind=kLoop, calls=%fused_computation.1 | loop fusion | flops 262144 | bytes 1572864 | tf_op jit(solution)/shard_map/convert_element_type | solution.py:805
  79.0 1.2 %slice_dynamic-update-slice_fusion = bf16[512,2048]{1,0:T(8,128)(2,1)S(1)} fusion(bf16[512,2560]{1,0:T(8,128)(2,1)} %get-tuple-element.9), kind=kLoop, calls=%fused_computation | loop fusion | bytes 1572864
  80.3 0.0 copy-done
  80.4 0.0 copy-start.2
  80.5 2.5 %convert_element_type.6 = f32[512,2048]{1,0:T(8,128)} convert(bf16[512,2048]{1,0:T(8,128)(2,1)S(1)} %slice_dynamic-update-slice_fusion.1) | non-fusion elementwise | flops 1048576 | bytes 6291456 | tf_op jit(solution)/shard_map/convert_element_type | solution.py:804
  83.0 0.0 copy-done.2
  83.0 0.0 copy-start.1
  83.0 0.9 %copy.21 = f32[384,512]{1,0:T(8,128)} copy(f32[384,512]{1,0:T(8,128)S(1)} %copy-done.2) | data formatting | bytes 1572864
  83.9 0.5 copy-done.1
  84.4 0.9 %copy.22 = f32[384,512]{1,0:T(8,128)} copy(f32[384,512]{1,0:T(8,128)S(1)} %copy-done.1) | data formatting | bytes 1572864
  (5 shorter events, 0.1 us)
Async XLA Ops:
  76.7 3.5 %copy-start = (bf16[512,2560]{1,0:T(8,128)(2,1)S(1)}, bf16[512,2560]{1,0:T(8,128)(2,1)}, u32[]{:S(2)}) copy-start(bf16[512,2560]{1,0:T(8,128)(2,1)} %get-tuple-element.9) | copy-start | bytes 7864324
  80.4 2.6 %copy-start.2 = (f32[384,512]{1,0:T(8,128)S(1)}, f32[384,512]{1,0:T(8,128)}, u32[]{:S(2)}) copy-start(f32[384,512]{1,0:T(8,128)} %get-tuple-element.14) | copy-start | bytes 2359300
  83.0 1.4 %copy-start.1 = (f32[384,512]{1,0:T(8,128)S(1)}, f32[384,512]{1,0:T(8,128)}, u32[]{:S(2)}) copy-start(f32[384,512]{1,0:T(8,128)} %get-tuple-element.15) | copy-start | bytes 2359300
